TPU v7x, 512 devices: a whole 4x4x16 slice. The times are simulated.
512 devices in a mesh: ep: 128 (over x, z, core), dp: 4 (over y).
Axes of the slice: x: 4, y: 4, z: 16, core: 2. Of those that a mesh axis runs over, the one named last changes fastest.
Arguments:
- tokens: bfloat16 [2, 2048, 2048], P(None, 'ep', 'dp'), may hold values from -6 to 6
- route_ids: int32 [2, 2048, 8], P(None, 'ep'), may hold values from 0 to 127, all different within a row; in each aligned block of 16 rows (0 to 15, 16 to 31, ..., all dimensions but the last counted through in order) at most 2 rows name the same one
- gate_vals: float32 [2, 2048, 8], P(None, 'ep'), may hold values from 0.05 to 1
- replica_choice: int32 [2, 128, 128], P(None, 'ep'), may hold values from 0 to 1
- placement: int32 [128, 2], replicated, may hold values from 0 to 127, as said below
- gate_up: bfloat16 [128, 2, 2048, 1536], P('ep', None, None, 'dp'), may hold values from -0.125 to 0.125
- down_proj: bfloat16 [128, 2, 768, 2048], P('ep', None, None, 'dp'), may hold values from -0.21875 to 0.21875
- changed_expert: int32 [128, 32], P('ep'), may hold values from 0 to 127, as said below
- changed_block: int32 [128, 32], P('ep'), may hold values from 0 to 255, as said below
- delta_gate_up: bfloat16 [128, 32, 8, 1536], P('ep', None, None, 'dp'), may hold values from -0.5 to 0.5
- delta_down: bfloat16 [128, 32, 3, 2048], P('ep', None, None, 'dp'), may hold values from -0.875 to 0.875
Outputs:
- layer_out: bfloat16 [2, 2048, 2048], P(None, 'ep', 'dp')
Inputs may be any that keep to these rules, and one draw needn't show every extreme that they name: `placement`: column 0 is a permutation of the experts (the primary replicas) and so is column 1 (the redundant ones); an expert's two replicas lie on different devices. `changed_expert`: the 32 experts listed by one learner are distinct. `changed_block`: each pair of an expert and a block number appears at most once among all learners' lists. `route_ids`: within the 16 tokens of one device at one step, no expert is named by more than 2 tokens.
All inputs are finite; a program needn't handle non-finite values.
Results may differ from a plain program's by a relative error of at most 0.0072.
Values may be sent and summed in bfloat16 or wider, within the bound.
No kernel may reach another device: no remote copies, remote signals or barrier semaphores. Data moves between devices by JAX's collectives and lax.ppermute only.
A program may use at most 128 MiB of HBM per device.

v0:
```python
import jax
import jax.numpy as jnp
from jax import lax
from jax.sharding import PartitionSpec as P

NBLK = 256


def refresh(
    gate_up, down_proj, placement, changed_expert, changed_block, delta_gate_up, delta_down
):
    ep_count = lax.axis_size("ep")
    changed_count = changed_expert.shape[1]
    block_count = NBLK
    flat_place = placement.reshape(ep_count * 2)
    matches = flat_place[:, None] == changed_expert[0][None, :]
    match_weights = matches.astype(jnp.bfloat16)
    gate_rows = delta_gate_up.reshape(changed_count, -1)
    down_rows = delta_down.reshape(changed_count, -1)
    send_gate = (
        jnp.dot(match_weights, gate_rows, preferred_element_type=jnp.float32)
        .astype(jnp.bfloat16)
        .reshape(ep_count, 2, -1)
    )
    send_down = (
        jnp.dot(match_weights, down_rows, preferred_element_type=jnp.float32)
        .astype(jnp.bfloat16)
        .reshape(ep_count, 2, -1)
    )
    labels = jnp.sum(jnp.where(matches, changed_block[0][None, :] + 1, 0), axis=1)
    send_labels = labels.astype(jnp.float32).astype(jnp.bfloat16).reshape(ep_count, 2)
    got_gate, got_down, got_labels = (
        lax.all_to_all(send_gate, "ep", split_axis=0, concat_axis=0, tiled=True),
        lax.all_to_all(send_down, "ep", split_axis=0, concat_axis=0, tiled=True),
        lax.all_to_all(send_labels, "ep", split_axis=0, concat_axis=0, tiled=True),
    )
    wanted = got_labels.astype(jnp.float32).T - 1.0
    block_ids = jnp.arange(block_count, dtype=jnp.float32)
    selector = (wanted[:, None, :] == block_ids[None, :, None]).astype(jnp.bfloat16)
    update_gate = jnp.einsum("jbn,njc->jbc", selector, got_gate, preferred_element_type=jnp.float32)
    update_down = jnp.einsum("jbn,njc->jbc", selector, got_down, preferred_element_type=jnp.float32)
    fresh_gate = (gate_up[0] + update_gate.reshape(gate_up.shape[1:])).astype(jnp.bfloat16)
    fresh_down = (down_proj[0] + update_down.reshape(down_proj.shape[1:])).astype(jnp.bfloat16)
    return (fresh_gate, fresh_down)


def slot_targets(route_step, choice_row, host, capacity):
    expert_count = choice_row.shape[0]
    flat_route = route_step.reshape(-1)
    expert_hits = (
        flat_route[:, None] == jnp.arange(expert_count, dtype=jnp.int32)[None, :]
    ).astype(jnp.int32)
    before = jnp.cumsum(expert_hits, axis=0) - expert_hits
    position = jnp.sum(before * expert_hits, axis=1)
    replica = jnp.sum(expert_hits * choice_row[None, :], axis=1)
    primary_host = jnp.sum(expert_hits * host[None, :, 0], axis=1)
    backup_host = jnp.sum(expert_hits * host[None, :, 1], axis=1)
    device_to = jnp.where(replica == 1, backup_host, primary_host)
    return ((device_to * 2 + replica) * capacity + position).reshape(route_step.shape)


def on_device(
    tokens,
    route_ids,
    gate_vals,
    replica_choice,
    placement,
    gate_up,
    down_proj,
    changed_expert,
    changed_block,
    delta_gate_up,
    delta_down,
):
    ep_count = lax.axis_size("ep")
    step_count = tokens.shape[0]
    row_count = tokens.shape[1]
    quarter = tokens.shape[2]
    top_count = route_ids.shape[2]
    expert_count = replica_choice.shape[2]
    capacity = min(row_count, max(2, 2 * row_count * top_count // expert_count))
    slot_total = ep_count * 2 * capacity
    fresh_gate, fresh_down = refresh(
        gate_up, down_proj, placement, changed_expert, changed_block, delta_gate_up, delta_down
    )
    half_hidden = fresh_gate.shape[2] // 2
    host = jnp.sum(
        jnp.arange(ep_count, dtype=jnp.int32)[:, None, None]
        * (
            placement[:, None, :] == jnp.arange(expert_count, dtype=jnp.int32)[None, :, None]
        ).astype(jnp.int32),
        axis=0,
    )
    source_rows = lax.all_gather(tokens, "dp", axis=2, tiled=True)
    send_width = source_rows.shape[2]

    def serve(received):
        mixed = jnp.einsum(
            "njcd,jdh->jnch", received, fresh_gate, preferred_element_type=jnp.float32
        )
        hidden = (jax.nn.silu(mixed[..., :half_hidden]) * mixed[..., half_hidden:]).astype(
            jnp.bfloat16
        )
        summed = jnp.einsum(
            "jnch,jhq->njcq",
            lax.all_gather(hidden, "dp", axis=3, tiled=True),
            fresh_down,
            preferred_element_type=jnp.float32,
        )
        return lax.all_to_all(
            summed.astype(jnp.bfloat16), "ep", split_axis=0, concat_axis=0, tiled=True
        )

    slot_ids = jnp.arange(slot_total, dtype=jnp.int32)
    targets = []
    sends = []
    for step_index in range(step_count):
        target = slot_targets(route_ids[step_index], replica_choice[step_index, 0], host, capacity)
        targets.append(target)
        picker = jnp.sum(
            (target[None, :, :] == slot_ids[:, None, None]).astype(jnp.int32), axis=2
        ).astype(jnp.bfloat16)
        packed = jnp.dot(
            picker, source_rows[step_index], preferred_element_type=jnp.float32
        ).astype(jnp.bfloat16)
        sends.append(packed.reshape(ep_count, 2, capacity, send_width))
    returned = [
        serve(lax.all_to_all(sends[step_index], "ep", split_axis=0, concat_axis=0, tiled=True))
        for step_index in range(step_count)
    ]
    outputs = []
    for step_index in range(step_count):
        target = targets[step_index]
        mixing = jnp.sum(
            jnp.where(
                target[:, :, None] == slot_ids[None, None, :],
                gate_vals[step_index][:, :, None],
                0.0,
            ),
            axis=1,
        )
        flat_back = returned[step_index].reshape(slot_total, quarter).astype(jnp.float32)
        combined = jnp.dot(mixing, flat_back, precision=lax.Precision.HIGHEST)
        outputs.append(combined.astype(jnp.bfloat16))
    return jnp.stack(outputs)


def solution(mesh):
    return jax.shard_map(
        on_device,
        mesh=mesh,
        in_specs=(
            P(None, "ep", "dp"),
            P(None, "ep", None),
            P(None, "ep", None),
            P(None, "ep", None),
            P(),
            P("ep", None, None, "dp"),
            P("ep", None, None, "dp"),
            P("ep", None),
            P("ep", None),
            P("ep", None, None, "dp"),
            P("ep", None, None, "dp"),
        ),
        out_specs=P(None, "ep", "dp"),
        check_vma=False,
    )
```

profile of v0, /device:TPU:40, one launch (start us, length us, event | category | flops | bytes accessed | tf_op | source)
XLA Modules:
  0.0 477.1 jit_solution(2153665191781665537)
XLA Ops:
  0.0 0.8 copy.66
  1.0 0.7 add_bitcast_fusion
  1.6 0.7 fusion.26
  2.4 0.8 convert_element_type.137
  3.2 19.0 %all-to-all-start = ((bf16[128,1,2]{2,1,0:T(2,128)(2,1)}), bf16[128,1,2]{2,1,0:T(2,128)(2,1)S(1)}, u32[]{:S(2)}, u32[]{:S(2)}) async-start(bf16[128,1,2]{2,1,0:T(2,128)(2,1)} %convert_element_type.137), calls=%async_computation | async-start | bytes 131072 | tf_op jit(solution)/shard_map/all_to_all | solution.py:35
  22.2 1.0 copy.69
  23.2 1.1 convolution_convert_fusion.3
  24.3 1.2 reshape.168
  25.5 11.8 %all-to-all-done = bf16[128,1,2]{2,1,0:T(2,128)(2,1)S(1)} async-done(((bf16[128,1,2]{2,1,0:T(2,128)(2,1)}), bf16[128,1,2]{2,1,0:T(2,128)(2,1)S(1)}, u32[]{:S(2)}, u32[]{:S(2)}) %all-to-all-start) | async-done | bytes 544 | tf_op jit(solution)/shard_map/all_to_all | solution.py:35
  37.3 6.5 %all-to-all-start.1 = ((bf16[128,2,1536]{2,1,0:T(2,128)(2,1)}), bf16[128,2,1536]{2,1,0:T(2,128)(2,1)S(1)}, u32[]{:S(2)}, u32[]{:S(2)}) async-start(bf16[128,2,1536]{2,1,0:T(2,128)(2,1)} %reshape.168), calls=%async_computation.1 | async-start | bytes 1572864 | tf_op jit(solution)/shard_map/all_to_all | solution.py:34
  43.9 0.7 convolution_convert_fusion
  44.6 1.6 reshape.172
  46.2 42.6 %all-to-all-done.1 = bf16[128,2,1536]{2,1,0:T(2,128)(2,1)S(1)} async-done(((bf16[128,2,1536]{2,1,0:T(2,128)(2,1)}), bf16[128,2,1536]{2,1,0:T(2,128)(2,1)S(1)}, u32[]{:S(2)}, u32[]{:S(2)}) %all-to-all-start.1) | async-done | bytes 786464 | tf_op jit(solution)/shard_map/all_to_all | solution.py:34
  88.8 7.1 %all-to-all-start.3 = ((bf16[128,2,3072]{2,1,0:T(2,128)(2,1)}), bf16[128,2,3072]{2,1,0:T(2,128)(2,1)}, u32[]{:S(2)}, u32[]{:S(2)}) async-start(bf16[128,2,3072]{2,1,0:T(2,128)(2,1)} %reshape.172), calls=%async_computation.3 | async-start | bytes 3145728 | tf_op jit(solution)/shard_map/all_to_all | solution.py:33
  96.9 0.3 select_reduce_fusion.8
  97.6 12.2 %all_gather.9 = bf16[2,16,2048]{2,1,0:T(8,128)(2,1)S(1)} all-gather(bf16[2,16,512]{2,1,0:T(8,128)(2,1)S(1)} %copy-done.1), channel_id=1, replica_groups=mesh['ep'=128,'dp'=4] {'dp'}, dimensions={2}, use_global_device_ids=true | all-gather | bytes 163840 | tf_op jit(solution)/shard_map/all_gather | solution.py:94
  110.0 0.7 convolution_convert_fusion.2
  110.7 2.7 reshape.170
  113.4 59.5 %all-to-all-done.3 = bf16[128,2,3072]{2,1,0:T(2,128)(2,1)} async-done(((bf16[128,2,3072]{2,1,0:T(2,128)(2,1)}), bf16[128,2,3072]{2,1,0:T(2,128)(2,1)}, u32[]{:S(2)}, u32[]{:S(2)}) %all-to-all-start.3) | async-done | bytes 1572896 | tf_op jit(solution)/shard_map/all_to_all | solution.py:33
  172.9 8.5 %all-to-all-start.2 = ((bf16[128,2,2,2048]{3,2,1,0:T(2,128)(2,1)}), bf16[128,2,2,2048]{3,2,1,0:T(2,128)(2,1)}, u32[]{:S(2)}, u32[]{:S(2)}) async-start(bf16[128,2,2,2048]{3,2,1,0:T(2,128)(2,1)} %reshape.170), calls=%async_computation.2 | async-start | bytes 4194304 | tf_op jit(solution)/shard_map/all_to_all | solution.py:128
  182.0 0.7 convolution_convert_fusion.1
  182.7 2.7 reshape.175
  185.4 95.4 %all-to-all-done.2 = bf16[128,2,2,2048]{3,2,1,0:T(2,128)(2,1)} async-done(((bf16[128,2,2,2048]{3,2,1,0:T(2,128)(2,1)}), bf16[128,2,2,2048]{3,2,1,0:T(2,128)(2,1)}, u32[]{:S(2)}, u32[]{:S(2)}) %all-to-all-start.2) | async-done | bytes 2097184 | tf_op jit(solution)/shard_map/all_to_all | solution.py:128
  280.8 8.6 %all-to-all-start.5 = ((bf16[128,2,2,2048]{3,2,1,0:T(2,128)(2,1)}), bf16[128,2,2,2048]{3,2,1,0:T(2,128)(2,1)}, u32[]{:S(2)}, u32[]{:S(2)}) async-start(bf16[128,2,2,2048]{3,2,1,0:T(2,128)(2,1)} %reshape.175), calls=%async_computation.5 | async-start | bytes 4194304 | tf_op jit(solution)/shard_map/all_to_all | solution.py:128
  289.5 2.3 fusion.16
  291.8 2.9 reshape.169
  294.7 5.1 %fusion.8 = f32[2,256,3072]{2,1,0:T(8,128)} fusion(bf16[128,2,3072]{2,1,0:T(2,128)(2,1)} %all-to-all-done.3, f32[2,128]{1,0:T(2,128)S(1)} %copy.68), kind=kOutput, calls=%fused_computation.14 | convolution fusion | flops 402718720 | bytes 7865344 | tf_op jit(solution)/shard_map/jbn,njc->jbc/dot_general | solution.py:40
  299.9 7.2 %reshape.173 = f32[2,2048,384]{2,1,0:T(8,128)} reshape(f32[2,256,3072]{2,1,0:T(8,128)} %fusion.8) | data formatting | bytes 12582912 | tf_op jit(solution)/shard_map/reshape | solution.py:42
  307.0 7.4 %fusion.5 = f32[2,128,2,384]{3,1,2,0:T(8,128)S(1)} fusion(bf16[128,2,2,2048]{3,2,1,0:T(2,128)(2,1)} %all-to-all-done.2, f32[2,2048,384]{2,1,0:T(8,128)} %reshape.173, bf16[1,2,2048,384]{3,2,1,0:T(8,128)(2,1)} %param.16), kind=kOutput, calls=%fused_computation.11 | convolution fusion | flops 810024960 | bytes 12320768 | tf_op jit(solution)/shard_map/njcd,jdh->jnch/dot_general | solution.py:98
  314.4 0.2 fusion.19
  314.6 0.8 copy.73
  315.5 14.4 %all_gather.10 = bf16[2,128,2,768]{1,2,0,3:T(2,128)(2,1)S(1)} all-gather(bf16[2,128,2,192]{1,2,0,3:T(2,128)(2,1)} %copy.73), channel_id=1, replica_groups=mesh['ep'=128,'dp'=4] {'dp'}, dimensions={3}, use_global_device_ids=true | all-gather | bytes 983040 | tf_op jit(solution)/shard_map/all_gather | solution.py:106
  329.9 3.0 fusion.10
  332.9 2.0 copy.76
  334.9 53.8 %all-to-all-done.5 = bf16[128,2,2,2048]{3,2,1,0:T(2,128)(2,1)} async-done(((bf16[128,2,2,2048]{3,2,1,0:T(2,128)(2,1)}), bf16[128,2,2,2048]{3,2,1,0:T(2,128)(2,1)}, u32[]{:S(2)}, u32[]{:S(2)}) %all-to-all-start.5) | async-done | bytes 2097184 | tf_op jit(solution)/shard_map/all_to_all | solution.py:128
  388.8 8.6 %all-to-all-start.4 = ((bf16[128,2,2,512]{3,2,1,0:T(2,128)(2,1)}), bf16[128,2,2,512]{3,2,1,0:T(2,128)(2,1)}, u32[]{:S(2)}, u32[]{:S(2)}) async-start(bf16[128,2,2,512]{3,2,1,0:T(2,128)(2,1)} %copy.76), calls=%async_computation.4 | async-start | bytes 1048576 | tf_op jit(solution)/shard_map/all_to_all | solution.py:110
  397.4 7.4 %fusion.3 = f32[2,128,2,384]{3,1,2,0:T(8,128)S(1)} fusion(bf16[128,2,2,2048]{3,2,1,0:T(2,128)(2,1)} %all-to-all-done.5, f32[2,2048,384]{2,1,0:T(8,128)} %reshape.173, bf16[1,2,2048,384]{3,2,1,0:T(8,128)(2,1)} %param.16), kind=kOutput, calls=%fused_computation.9 | convolution fusion | flops 810024960 | bytes 12320768 | tf_op jit(solution)/shard_map/njcd,jdh->jnch/dot_general | solution.py:98
  405.0 0.8 copy.80
  405.8 14.4 %all_gather.11 = bf16[2,128,2,768]{1,2,0,3:T(2,128)(2,1)S(1)} all-gather(bf16[2,128,2,192]{1,2,0,3:T(2,128)(2,1)} %copy.80), channel_id=1, replica_groups=mesh['ep'=128,'dp'=4] {'dp'}, dimensions={3}, use_global_device_ids=true | all-gather | bytes 983040 | tf_op jit(solution)/shard_map/all_gather | solution.py:106
  420.2 3.0 fusion.11
  423.3 2.0 copy.83
  425.3 6.2 %all-to-all-done.4 = bf16[128,2,2,512]{3,2,1,0:T(2,128)(2,1)} async-done(((bf16[128,2,2,512]{3,2,1,0:T(2,128)(2,1)}), bf16[128,2,2,512]{3,2,1,0:T(2,128)(2,1)}, u32[]{:S(2)}, u32[]{:S(2)}) %all-to-all-start.4) | async-done | bytes 524320 | tf_op jit(solution)/shard_map/all_to_all | solution.py:110
  431.5 10.0 %all-to-all-start.6 = ((bf16[128,2,2,512]{3,2,1,0:T(2,128)(2,1)}), bf16[128,2,2,512]{3,2,1,0:T(2,128)(2,1)S(1)}, u32[]{:S(2)}, u32[]{:S(2)}) async-start(bf16[128,2,2,512]{3,2,1,0:T(2,128)(2,1)} %copy.83), calls=%async_computation.6 | async-start | bytes 1048576 | tf_op jit(solution)/shard_map/all_to_all | solution.py:110
  442.0 1.2 reshape.174
  443.2 0.3 fusion.12
  443.5 32.4 %all-to-all-done.6 = bf16[128,2,2,512]{3,2,1,0:T(2,128)(2,1)S(1)} async-done(((bf16[128,2,2,512]{3,2,1,0:T(2,128)(2,1)}), bf16[128,2,2,512]{3,2,1,0:T(2,128)(2,1)S(1)}, u32[]{:S(2)}, u32[]{:S(2)}) %all-to-all-start.6) | async-done | bytes 524320 | tf_op jit(solution)/shard_map/all_to_all | solution.py:110
  476.1 0.3 fusion.13
  476.5 0.6 pad_maximum_fusion
  (51 shorter events, 3.2 us)
Async XLA Ops:
  0.0 43.9 %copy-start.4 = (s32[1,32]{1,0:T(1,128)S(1)}, s32[1,32]{1,0:T(1,128)}, u32[]{:S(2)}) copy-start(s32[1,32]{1,0:T(1,128)} %param.18) | copy-start | bytes 388
  0.0 43.8 %copy-start = (bf16[1,32,8,384]{3,2,1,0:T(8,128)(2,1)S(1)}, bf16[1,32,8,384]{3,2,1,0:T(8,128)(2,1)}, u32[]{:S(2)}) copy-start(bf16[1,32,8,384]{3,2,1,0:T(8,128)(2,1)} %param.20) | copy-start | bytes 589828
  3.2 34.1 %all-to-all-start = ((bf16[128,1,2]{2,1,0:T(2,128)(2,1)}), bf16[128,1,2]{2,1,0:T(2,128)(2,1)S(1)}, u32[]{:S(2)}, u32[]{:S(2)}) async-start(bf16[128,1,2]{2,1,0:T(2,128)(2,1)} %convert_element_type.137), calls=%async_computation | async-start | bytes 131072 | tf_op jit(solution)/shard_map/all_to_all | solution.py:35
  37.3 51.5 %all-to-all-start.1 = ((bf16[128,2,1536]{2,1,0:T(2,128)(2,1)}), bf16[128,2,1536]{2,1,0:T(2,128)(2,1)S(1)}, u32[]{:S(2)}, u32[]{:S(2)}) async-start(bf16[128,2,1536]{2,1,0:T(2,128)(2,1)} %reshape.168), calls=%async_computation.1 | async-start | bytes 1572864 | tf_op jit(solution)/shard_map/all_to_all | solution.py:34
  44.6 51.4 %copy-start.2 = (s32[2,16,8]{1,2,0:T(8,128)S(1)}, s32[2,16,8]{1,2,0:T(8,128)}, u32[]{:S(2)}) copy-start(s32[2,16,8]{1,2,0:T(8,128)} %param.12) | copy-start | bytes 3076
  44.6 52.2 %copy-start.5 = (s32[128,2]{0,1:T(2,128)S(1)}, s32[128,2]{0,1:T(2,128)}, u32[]{:S(2)}) copy-start(s32[128,2]{0,1:T(2,128)} %param.15) | copy-start | bytes 3076
  44.6 52.3 %copy-start.6 = (s32[2,1,128]{2,1,0:T(1,128)S(1)}, s32[2,1,128]{2,1,0:T(1,128)}, u32[]{:S(2)}) copy-start(s32[2,1,128]{2,1,0:T(1,128)} %param.14) | copy-start | bytes 3076
  44.6 53.0 %copy-start.1 = (bf16[2,16,512]{2,1,0:T(8,128)(2,1)S(1)}, bf16[2,16,512]{2,1,0:T(8,128)(2,1)}, u32[]{:S(2)}) copy-start(bf16[2,16,512]{2,1,0:T(8,128)(2,1)} %param.11) | copy-start | bytes 98308
  88.8 84.1 %all-to-all-start.3 = ((bf16[128,2,3072]{2,1,0:T(2,128)(2,1)}), bf16[128,2,3072]{2,1,0:T(2,128)(2,1)}, u32[]{:S(2)}, u32[]{:S(2)}) async-start(bf16[128,2,3072]{2,1,0:T(2,128)(2,1)} %reshape.172), calls=%async_computation.3 | async-start | bytes 3145728 | tf_op jit(solution)/shard_map/all_to_all | solution.py:33
  172.9 107.9 %all-to-all-start.2 = ((bf16[128,2,2,2048]{3,2,1,0:T(2,128)(2,1)}), bf16[128,2,2,2048]{3,2,1,0:T(2,128)(2,1)}, u32[]{:S(2)}, u32[]{:S(2)}) async-start(bf16[128,2,2,2048]{3,2,1,0:T(2,128)(2,1)} %reshape.170), calls=%async_computation.2 | async-start | bytes 4194304 | tf_op jit(solution)/shard_map/all_to_all | solution.py:128
  280.8 108.0 %all-to-all-start.5 = ((bf16[128,2,2,2048]{3,2,1,0:T(2,128)(2,1)}), bf16[128,2,2,2048]{3,2,1,0:T(2,128)(2,1)}, u32[]{:S(2)}, u32[]{:S(2)}) async-start(bf16[128,2,2,2048]{3,2,1,0:T(2,128)(2,1)} %reshape.175), calls=%async_computation.5 | async-start | bytes 4194304 | tf_op jit(solution)/shard_map/all_to_all | solution.py:128
  388.8 42.7 %all-to-all-start.4 = ((bf16[128,2,2,512]{3,2,1,0:T(2,128)(2,1)}), bf16[128,2,2,512]{3,2,1,0:T(2,128)(2,1)}, u32[]{:S(2)}, u32[]{:S(2)}) async-start(bf16[128,2,2,512]{3,2,1,0:T(2,128)(2,1)} %copy.76), calls=%async_computation.4 | async-start | bytes 1048576 | tf_op jit(solution)/shard_map/all_to_all | solution.py:110
  420.2 21.2 %copy-start.3 = (f32[2,16,8]{1,2,0:T(8,128)S(1)}, f32[2,16,8]{1,2,0:T(8,128)}, u32[]{:S(2)}) copy-start(f32[2,16,8]{1,2,0:T(8,128)} %param.13) | copy-start | bytes 3076
  431.5 44.5 %all-to-all-start.6 = ((bf16[128,2,2,512]{3,2,1,0:T(2,128)(2,1)}), bf16[128,2,2,512]{3,2,1,0:T(2,128)(2,1)S(1)}, u32[]{:S(2)}, u32[]{:S(2)}) async-start(bf16[128,2,2,512]{3,2,1,0:T(2,128)(2,1)} %copy.83), calls=%async_computation.6 | async-start | bytes 1048576 | tf_op jit(solution)/shard_map/all_to_all | solution.py:110
where the time goes:
time: 478 us; the launch traced here: 477 us
  waiting for transfers between devices  302 us (63%)
  starting transfers between devices  68.4 us (14%)
  blocking collectives  41.1 us (9%)
  matrix products  32.1 us (7%)
  local copies, waits for them, and re-layouts  29.3 us (6%)
    all_to_all x2, waiting for transfers between devices, on_device(): lax.all_to_all(sends[step_index], 'ep', split_axis=0, concat_axis=0, tile...  149 us
    all_to_all x1, waiting for transfers between devices, refresh(): lax.all_to_all(send_gate, 'ep', split_axis=0, concat_axis=0, tiled=True)  59.5 us
    all_to_all x1, waiting for transfers between devices, refresh(): lax.all_to_all(send_down, 'ep', split_axis=0, concat_axis=0, tiled=True)  42.6 us
    all_to_all x2, waiting for transfers between devices, serve(): lax.all_to_all(summed.astype(jnp.bfloat16), 'ep', split_axis=0, concat_ax...  38.6 us
    all_gather x2, blocking collectives, serve(): lax.all_gather(hidden, 'dp', axis=3, tiled=True)  28.9 us
    all_to_all x1, starting transfers between devices, refresh(): lax.all_to_all(send_labels, 'ep', split_axis=0, concat_axis=0, tiled=True)  19 us
    all_to_all x2, starting transfers between devices, serve(): lax.all_to_all(summed.astype(jnp.bfloat16), 'ep', split_axis=0, concat_ax...  18.6 us
    all_to_all x2, starting transfers between devices, on_device(): lax.all_to_all(sends[step_index], 'ep', split_axis=0, concat_axis=0, tile...  17.1 us
  transfers between devices with their start and end apart: 7, of which 7 were waited for; matrix products, arithmetic and copies ran while one was open for 13% of the time, Pallas kernels for 0%

commit v1 on v0

v1 whole, which is shorter than its diff:
```python
import functools

import jax
import jax.numpy as jnp
from jax import lax
from jax.experimental import pallas as pl
from jax.experimental.pallas import tpu as pltpu
from jax.sharding import Mesh, PartitionSpec as P

NX = 4
NC = 2
EP = ("x", "z", "c")
XC = ("x", "c")
CAP = 2
META = 128
BF = jnp.bfloat16
F32 = jnp.float32
PARAMS = pltpu.CompilerParams(vmem_limit_bytes=40 * 1024 * 1024)


def slot_codes(route, choice, placement):
    steps, rows, top = route.shape
    experts = choice.shape[1]
    devices = placement.shape[0]
    expert_ids = jnp.arange(experts, dtype=jnp.int32)
    device_ids = jnp.arange(devices, dtype=jnp.int32)
    host = jnp.sum(
        jnp.where(placement[:, :, None] == expert_ids, device_ids[:, None, None], 0), axis=0
    )
    table = jnp.where(choice == 1, host[1] * 2 + 1, host[0] * 2)
    flat = route.reshape(steps, rows * top)
    slot = jnp.sum(
        jnp.where(flat[:, :, None] == expert_ids, table[:, None, :], 0), axis=2
    )
    order = jnp.arange(rows * top, dtype=jnp.int32)
    position = jnp.sum(
        ((flat[:, :, None] == flat[:, None, :]) & (order[None, :] < order[:, None])).astype(
            jnp.int32
        ),
        axis=2,
    )
    return (slot * CAP + position - devices * CAP).reshape(steps, rows, top)


def pick_kernel(tok_ref, code_ref, target_ref, label_ref, out_ref):
    zs, rows2, _ = tok_ref.shape
    peers, _, width = out_ref.shape
    steps, top, count = code_ref.shape
    rows = rows2 // steps
    slots = target_ref.shape[0]
    part = slots // (peers * 2)
    own = lax.broadcasted_iota(jnp.int32, (slots, count), 0) % part // CAP
    held = lax.broadcasted_iota(jnp.int32, (slots, count), 1) // rows
    same = own == held
    target = target_ref[...]
    for s in range(steps):
        hit = code_ref[s, 0:1, :] == target
        for k in range(1, top):
            hit = hit | (code_ref[s, k : k + 1, :] == target)
        pick = jnp.where(hit & same, 1.0, 0.0).astype(BF)
        toks = tok_ref[:, s * rows : (s + 1) * rows, :width].reshape(count, width)
        got = jnp.dot(pick, toks, preferred_element_type=F32).astype(BF)
        got = got.reshape(peers, 2, part, width)
        for j in range(2):
            start = (j * steps + s) * part
            out_ref[:, start : start + part, :] = got[:, j]
    out_ref[:, 2 * steps * part :, :] = label_ref[...]


def pick_rows(packets, codes_t, target_col, labels, width, peers, rows):
    return pl.pallas_call(
        pick_kernel,
        out_shape=jax.ShapeDtypeStruct((peers, rows + 16, width), BF),
        compiler_params=PARAMS,
        cost_estimate=pl.CostEstimate(
            flops=4 * codes_t.shape[2] * target_col.shape[0] * width,
            bytes_accessed=4 * 1024 * 1024,
            transcendentals=0,
        ),
    )(packets, codes_t, target_col, labels)


def gate_kernel(br, where_ref, w_ref, d_ref, t_ref, *refs):
    tok_refs, out_ref, cat_ref = refs[:-2], refs[-2], refs[-1]
    peers, zs, _ = d_ref.shape
    depth, cols = w_ref.shape[1:]
    learners = peers * zs
    quarter = tok_refs[0].shape[2]
    parts = len(tok_refs)
    for r in range(br):
        cat_ref[r * learners : (r + 1) * learners, :] = d_ref[
            :, :, r * cols : (r + 1) * cols
        ].reshape(learners, cols)
    chunk = min(256, quarter)
    row_ids = lax.broadcasted_iota(jnp.int32, (chunk, br * learners), 0)
    tgt = t_ref[0]
    acc = None
    for n in range(parts):
        q = where_ref[n]
        for c in range(quarter // chunk):
            base = pl.multiple_of(q * quarter + c * chunk, chunk)
            spread = jnp.where(row_ids == tgt - base, 1.0, 0.0).astype(BF)
            update = jnp.dot(spread, cat_ref[...], preferred_element_type=F32)
            fresh = (w_ref[0, pl.ds(base, chunk), :].astype(F32) + update).astype(BF)
            toks = tok_refs[n][:, :, c * chunk : (c + 1) * chunk].reshape(-1, chunk)
            term = jnp.dot(toks, fresh, preferred_element_type=F32)
            acc = term if acc is None else acc + term
    half = cols // 2
    up = pltpu.roll(acc, half, 1)
    act = acc / (1.0 + jnp.exp(-acc)) * up
    out_ref[0] = act[:, :half].astype(BF)


def gate_hidden(where, gate_up, deltas, targets, toks, br):
    _, depth, cols = gate_up.shape
    peers, rows, quarter = toks[0].shape
    zs = deltas.shape[1] // 2
    slot_rows = peers * rows // 2
    learners = peers * zs
    grid_spec = pltpu.PrefetchScalarGridSpec(
        num_scalar_prefetch=1,
        grid=(2,),
        in_specs=[
            pl.BlockSpec((1, depth, cols), lambda j, w: (j, 0, 0)),
            pl.BlockSpec((peers, zs, deltas.shape[2]), lambda j, w: (0, j, 0)),
            pl.BlockSpec((1, 1, br * learners), lambda j, w: (j, 0, 0)),
        ]
        + [pl.BlockSpec((peers, rows // 2, quarter), lambda j, w: (0, j, 0))] * len(toks),
        out_specs=pl.BlockSpec((1, slot_rows, cols // 2), lambda j, w: (j, 0, 0)),
        scratch_shapes=[pltpu.VMEM((br * learners, cols), BF)],
    )
    return pl.pallas_call(
        functools.partial(gate_kernel, br),
        grid_spec=grid_spec,
        out_shape=jax.ShapeDtypeStruct((2, slot_rows, cols // 2), BF),
        compiler_params=PARAMS,
        cost_estimate=pl.CostEstimate(
            flops=4 * depth * cols * (slot_rows + br * learners),
            bytes_accessed=10 * 1024 * 1024,
            transcendentals=2 * slot_rows * cols,
        ),
    )(where, gate_up, deltas, targets, *toks)


def down_kernel(br, w_ref, d_ref, t_ref, out_ref, cat_ref):
    peers, zs, _ = d_ref.shape
    depth, cols = w_ref.shape[1:]
    learners = peers * zs
    for r in range(br):
        cat_ref[r * learners : (r + 1) * learners, :] = d_ref[
            :, :, r * cols : (r + 1) * cols
        ].reshape(learners, cols)
    row_ids = lax.broadcasted_iota(jnp.int32, (depth, br * learners), 0)
    spread = jnp.where(row_ids == t_ref[0], 1.0, 0.0).astype(BF)
    update = jnp.dot(spread, cat_ref[...], preferred_element_type=F32)
    out_ref[0] = (w_ref[0].astype(F32) + update).astype(BF)


def fresh_down(down, deltas, targets, br):
    _, depth, cols = down.shape
    peers, zs = deltas.shape[0], deltas.shape[1] // 2
    learners = peers * zs
    return pl.pallas_call(
        functools.partial(down_kernel, br),
        grid=(2,),
        in_specs=[
            pl.BlockSpec((1, depth, cols), lambda j: (j, 0, 0)),
            pl.BlockSpec((peers, zs, deltas.shape[2]), lambda j: (0, j, 0)),
            pl.BlockSpec((1, 1, br * learners), lambda j: (j, 0, 0)),
        ],
        out_specs=pl.BlockSpec((1, depth, cols), lambda j: (j, 0, 0)),
        scratch_shapes=[pltpu.VMEM((br * learners, cols), BF)],
        out_shape=jax.ShapeDtypeStruct((2, depth, cols), BF),
        compiler_params=PARAMS,
        cost_estimate=pl.CostEstimate(
            flops=4 * depth * cols * br * learners,
            bytes_accessed=5 * 1024 * 1024,
            transcendentals=0,
        ),
    )(down, deltas, targets)


def out_kernel(peers, h0_ref, h1_ref, w_ref, out_ref):
    parts, slot_rows, hd = h0_ref.shape
    cols = w_ref.shape[2]
    for j, h_ref in enumerate((h0_ref, h1_ref)):
        acc = None
        for p in range(parts):
            term = jnp.dot(
                h_ref[p], w_ref[j, p * hd : (p + 1) * hd, :], preferred_element_type=F32
            )
            acc = term if acc is None else acc + term
        out_ref[:, j] = acc.astype(BF).reshape(peers, slot_rows // peers, cols)


def expert_out(h0, h1, down, peers):
    parts, slot_rows, hd = h0.shape
    cols = down.shape[2]
    return pl.pallas_call(
        functools.partial(out_kernel, peers),
        out_shape=jax.ShapeDtypeStruct((peers, 2, slot_rows // peers, cols), BF),
        compiler_params=PARAMS,
        cost_estimate=pl.CostEstimate(
            flops=4 * slot_rows * cols * parts * hd,
            bytes_accessed=5 * 1024 * 1024,
            transcendentals=0,
        ),
    )(h0, h1, down)


def mix_kernel(ret_ref, code_ref, gate_ref, target_ref, out_ref):
    peers, _, steps, part, width = ret_ref.shape
    _, count, top = code_ref.shape
    zs, rows2, _ = out_ref.shape
    rows = rows2 // steps
    slots = peers * 2 * part
    own = lax.broadcasted_iota(jnp.int32, (count, slots), 1) % part // CAP
    held = lax.broadcasted_iota(jnp.int32, (count, slots), 0) // rows
    same = own == held
    target = target_ref[...]
    for s in range(steps):
        weight = jnp.zeros((count, slots), F32)
        for k in range(top):
            hit = code_ref[s, :, k : k + 1] == target
            weight = jnp.where(hit, gate_ref[s, :, k : k + 1], weight)
        weight = jnp.where(same, weight, 0.0)
        back = ret_ref[:, :, s].reshape(slots, width)
        high = weight.astype(BF)
        rest = weight - high.astype(F32)
        mid = rest.astype(BF)
        low = (rest - mid.astype(F32)).astype(BF)
        total = (
            jnp.dot(high, back, preferred_element_type=F32)
            + jnp.dot(mid, back, preferred_element_type=F32)
            + jnp.dot(low, back, preferred_element_type=F32)
        )
        out_ref[:, s * rows : (s + 1) * rows, :] = total.astype(BF).reshape(zs, rows, width)


def mix_rows(back, codes, gates, target_row, zs, rows2):
    width = back.shape[-1]
    return pl.pallas_call(
        mix_kernel,
        out_shape=jax.ShapeDtypeStruct((zs, rows2, width), BF),
        compiler_params=PARAMS,
        cost_estimate=pl.CostEstimate(
            flops=12 * codes.shape[1] * target_row.shape[1] * width,
            bytes_accessed=2 * 1024 * 1024,
            transcendentals=0,
        ),
    )(back, codes, gates, target_row)


def on_device(
    tokens,
    route_ids,
    gate_vals,
    replica_choice,
    placement,
    gate_up,
    down_proj,
    changed_expert,
    changed_block,
    delta_gate_up,
    delta_down,
):
    nx, nz, nc, nd = (lax.axis_size(a) for a in ("x", "z", "c", "dp"))
    peers = nx * nc
    steps, rows, quarter = tokens.shape
    top = route_ids.shape[2]
    changed, br, gate_cols = delta_gate_up.shape[1:]
    br2, down_cols = delta_down.shape[2:]
    z = lax.axis_index("z")
    p = lax.axis_index("dp")

    flat_deltas = jnp.concatenate(
        [delta_gate_up.reshape(changed, -1), delta_down.reshape(changed, -1)], axis=1
    )
    deltas = lax.all_gather(flat_deltas, "z", axis=0, tiled=True)

    codes = slot_codes(route_ids, replica_choice[:, 0], placement)
    high = lax.reduce_precision(gate_vals, 8, 7)
    mid = lax.reduce_precision(gate_vals - high, 8, 7)
    low = gate_vals - high - mid
    meta = jnp.concatenate([codes.astype(F32), high, mid, low], axis=2).reshape(
        steps * rows, 4 * top
    )
    names = jnp.stack([changed_expert[0], changed_block[0]], axis=1).astype(F32)
    meta = jnp.concatenate([meta, names], axis=1)
    meta = jnp.pad(meta, ((0, 0), (0, META - meta.shape[1]))).astype(BF)
    packet = jnp.concatenate([tokens.reshape(steps * rows, quarter), meta], axis=1)
    packets = lax.all_gather(packet, "z", axis=0, tiled=False)

    metas = packets[:, :, quarter:].astype(F32)
    gathered = metas.reshape(nz, steps, rows, META).transpose(1, 0, 2, 3)
    gathered = gathered.reshape(steps, nz * rows, META)
    codes_all = gathered[:, :, :top]
    gates_all = (
        gathered[:, :, top : 2 * top]
        + gathered[:, :, 2 * top : 3 * top]
        + gathered[:, :, 3 * top : 4 * top]
    )
    codes_t = codes_all.transpose(0, 2, 1)
    names_expert = metas[:, :, 4 * top]
    names_block = metas[:, :, 4 * top + 1]

    devs = (
        jnp.arange(nx, dtype=jnp.int32)[:, None] * nz + z
    ) * nc + jnp.arange(nc, dtype=jnp.int32)[None, :]
    devs = devs.reshape(peers)
    slot_ids = devs[:, None] * 2 + jnp.arange(2, dtype=jnp.int32)[None, :]
    target = slot_ids[:, :, None, None] * CAP + jnp.arange(CAP, dtype=jnp.int32)
    target = jnp.broadcast_to(target, (peers, 2, nz, CAP)).reshape(-1)
    target = (target - nx * nz * nc * CAP).astype(F32)

    held = lax.dynamic_index_in_dim(
        placement.reshape(nx, nz, nc, 2), z, axis=1, keepdims=False
    ).reshape(peers, 2)
    held = held.astype(F32)
    match = held[:, :, None, None] == names_expert[None, None]
    labels = jnp.sum(jnp.where(match, names_block + 1.0, 0.0), axis=3)
    labels = labels.reshape(peers, 1, 2 * nz).astype(BF)
    labels = jnp.pad(labels, ((0, 0), (0, 15), (0, quarter - 2 * nz)))
    z_ids = jnp.arange(nz, dtype=jnp.int32)
    chosen = (
        match[:, :, None, :, :] & (z_ids[:, None] == z_ids[None, :])[None, None, :, :, None]
    )
    chosen = chosen.astype(BF).reshape(peers * 2 * nz, nz * changed)

    count_rows = 2 * steps * nz * CAP
    picked = pick_rows(
        packets, codes_t, target[:, None], labels, quarter, peers, count_rows
    )
    got = lax.all_to_all(picked, XC, split_axis=0, concat_axis=0, tiled=True)
    own = got[:, :count_rows]
    toks = [own] + [
        lax.ppermute(own, "dp", [(i, (i + n) % nd) for i in range(nd)]) for n in range(1, nd)
    ]
    where = jnp.stack([(p - n) % nd for n in range(nd)]).astype(jnp.int32)
    block_of = got[:, count_rows, : 2 * nz].astype(F32).astype(jnp.int32) - 1
    block_of = block_of.reshape(peers, 2, nz).transpose(1, 0, 2).reshape(2, 1, peers * nz)
    gate_targets = (block_of * br + jnp.arange(br, dtype=jnp.int32)[None, :, None]).reshape(
        2, 1, -1
    )
    down_targets = (block_of * br2 + jnp.arange(br2, dtype=jnp.int32)[None, :, None]).reshape(
        2, 1, -1
    )

    cut = br * gate_cols
    deltas, _ = lax.optimization_barrier((deltas, own))
    send_gate = jnp.dot(chosen, deltas[:, :cut], preferred_element_type=F32).astype(BF)
    got_gate = lax.all_to_all(
        send_gate.reshape(peers, 2 * nz, cut), XC, split_axis=0, concat_axis=0, tiled=True
    )
    got_gate, deltas = lax.optimization_barrier((got_gate, deltas))
    send_down = jnp.dot(chosen, deltas[:, cut:], preferred_element_type=F32).astype(BF)
    got_down = lax.all_to_all(
        send_down.reshape(peers, 2 * nz, br2 * down_cols),
        XC,
        split_axis=0,
        concat_axis=0,
        tiled=True,
    )

    hidden = gate_hidden(where, gate_up[0], got_gate, gate_targets, toks, br)
    down = fresh_down(down_proj[0], got_down, down_targets, br2)
    h0 = lax.all_gather(hidden[0], "dp", axis=0, tiled=False)
    h1 = lax.all_gather(hidden[1], "dp", axis=0, tiled=False)
    out = expert_out(h0, h1, down, peers).reshape(peers, count_rows, down_cols)

    back = lax.all_to_all(out, XC, split_axis=0, concat_axis=0, tiled=True)
    back = back.reshape(peers, 2, steps, nz * CAP, down_cols)
    partial = mix_rows(back, codes_all, gates_all, target[None, :], nz, steps * rows)
    final = lax.all_to_all(partial, "z", split_axis=0, concat_axis=0, tiled=True)
    total = jnp.sum(final.astype(F32), axis=0).astype(BF)
    return total.reshape(steps, rows, down_cols)


def solution(mesh):
    ep, nd = mesh.devices.shape
    cube = Mesh(mesh.devices.reshape(NX, ep // (NX * NC), NC, nd), EP + ("dp",))
    return jax.shard_map(
        on_device,
        mesh=cube,
        in_specs=(
            P(None, EP, "dp"),
            P(None, EP, None),
            P(None, EP, None),
            P(None, EP, None),
            P(),
            P(EP, None, None, "dp"),
            P(EP, None, None, "dp"),
            P(EP, None),
            P(EP, None),
            P(EP, None, None, "dp"),
            P(EP, None, None, "dp"),
        ),
        out_specs=P(None, EP, "dp"),
        check_vma=False,
    )
```

time: 478 us -> 274 us (0.57)
  the two profiles are of different devices: /device:TPU:40 before, /device:TPU:8 now
where the time goes in v1:
time: 274 us; the launch traced here: 273 us
  blocking collectives  106 us (39%)
  waiting for transfers between devices  81.3 us (30%)
  starting transfers between devices  27.7 us (10%)
  Pallas kernels  18.6 us (7%)
  local copies, waits for them, and re-layouts  13.7 us (5%)
  between operations  13.7 us (5%)
  matrix products  6.94 us (3%)
  other arithmetic  5.48 us (2%)
    all_gather x1, blocking collectives, on_device(): packets = lax.all_gather(packet, 'z', axis=0, tiled=False)  42.4 us
    all_to_all x1, blocking collectives, on_device(): lax.all_to_all(partial, 'z', split_axis=0, concat_axis=0, tiled=True)  35.6 us
    ppermute x3, waiting for transfers between devices, on_device(): lax.ppermute(own, 'dp', [(i, (i + n) % nd) for i in range(nd)])  27.3 us
    all_to_all x1, waiting for transfers between devices, on_device(): got = lax.all_to_all(picked, XC, split_axis=0, concat_axis=0, tiled=True)  16 us
    all_to_all x1, waiting for transfers between devices, on_device(): back = lax.all_to_all(out, XC, split_axis=0, concat_axis=0, tiled=True)  15.8 us
    all_gather x1, waiting for transfers between devices, on_device(): deltas = lax.all_gather(flat_deltas, 'z', axis=0, tiled=True)  15.2 us
    all_gather x1, blocking collectives, on_device(): h1 = lax.all_gather(hidden[1], 'dp', axis=0, tiled=False)  14.2 us
    all_gather x1, blocking collectives, on_device(): h0 = lax.all_gather(hidden[0], 'dp', axis=0, tiled=False)  13.4 us
  transfers between devices with their start and end apart: 8, of which 7 were waited for; matrix products, arithmetic and copies ran while one was open for 6% of the time, Pallas kernels for 5%

profile of v1, /device:TPU:8, one launch (start us, length us, event | category | flops | bytes accessed | tf_op | source)
XLA Modules:
  0.0 273.0 jit_solution(12108632970222917098)
XLA Ops:
  6.6 1.0 copy.73
  7.7 1.0 copy.87
  8.6 0.7 pad_maximum_fusion
  9.9 0.2 select_reduce_fusion.1
  10.8 42.4 %all-gather = bf16[512,640]{1,0:T(8,128)(2,1)S(1)} all-gather(bf16[32,640]{1,0:T(8,128)(2,1)S(1)} %pad_maximum_fusion.1), channel_id=2, replica_groups=mesh['x'=4,'z'=16,'c'=2,'dp'=4] {'z'}, dimensions={0}, use_global_device_ids=true | all-gather | bytes 696320 | tf_op jit(solution)/shard_map/all_gather | solution.py:292
  53.2 0.4 fusion.2
  53.5 0.2 select_reduce_fusion
  53.9 0.3 slice_add_fusion
  54.7 2.1 shard_map.109
  56.8 4.5 %all-to-all-start = ((bf16[8,144,512]{2,1,0:T(8,128)(2,1)}), bf16[8,144,512]{2,1,0:T(8,128)(2,1)S(1)}, u32[]{:S(2)}, u32[]{:S(2)}) async-start(bf16[8,144,512]{2,1,0:T(8,128)(2,1)} %shard_map.109), calls=%async_computation | async-start | bytes 2359296 | tf_op jit(solution)/shard_map/all_to_all | solution.py:334
  61.4 0.4 broadcast_and_fusion
  61.7 0.9 and.53
  62.6 16.0 %all-to-all-done = bf16[8,144,512]{2,1,0:T(8,128)(2,1)S(1)} async-done(((bf16[8,144,512]{2,1,0:T(8,128)(2,1)}), bf16[8,144,512]{2,1,0:T(8,128)(2,1)S(1)}, u32[]{:S(2)}, u32[]{:S(2)}) %all-to-all-start) | async-done | bytes 1179680 | tf_op jit(solution)/shard_map/all_to_all | solution.py:334
  78.6 1.1 slice.64.refs_0_
  79.7 15.2 %all-gather.3.cloned.1.call-done = bf16[512,4608]{1,0:T(8,128)(2,1)} async-done(((bf16[32,4608]{1,0:T(8,128)(2,1)}), bf16[512,4608]{1,0:T(8,128)(2,1)}) %all-gather.3.cloned.1.call-update) | async-done | bytes 4718608 | tf_op jit(solution)/shard_map/all_gather | solution.py:279
  94.9 4.0 %convolution_convert_fusion = bf16[256,3072]{1,0:T(8,128)(2,1)} fusion(pred[256,512]{1,0:T(32,128)(4,1)S(1)} %and.53, bf16[512,4608]{1,0:T(8,128)(2,1)} %all-gather.3.cloned.1.call-done), kind=kOutput, calls=%fused_computation | convolution fusion | flops 806092800 | bytes 4849664 | tf_op jit(solution)/shard_map/dot_general | solution.py:351
  99.0 4.7 %all-to-all-start.1 = ((bf16[8,32,3072]{2,1,0:T(8,128)(2,1)}), bf16[8,32,3072]{2,1,0:T(8,128)(2,1)S(1)}, u32[]{:S(2)}, u32[]{:S(2)}) async-start(bf16[8,32,3072]{2,1,0:T(8,128)(2,1)} %bitcast.62), calls=%async_computation.1 | async-start | bytes 3145728 | tf_op jit(solution)/shard_map/all_to_all | solution.py:352
  103.6 0.5 iota_bitcast_fusion.1
  104.2 3.4 %collective-permute-start = (bf16[8,128,512]{2,1,0:T(8,128)(2,1)}, bf16[8,128,512]{2,1,0:T(8,128)(2,1)}, u32[]{:S(2)}, u32[]{:S(2)}) collective-permute-start(bf16[8,128,512]{2,1,0:T(8,128)(2,1)} %slice.64.refs_0_), channel_id=1, source_target_pairs={{0,1},{1,2},{2,3},{3,0},{4,5},{5,6},{6,7},{7,4},{8,9},{9,10},{10,1... | collective-permute-start | bytes 3145736 | tf_op jit(solution)/shard_map/ppermute | solution.py:337
  107.5 3.1 %collective-permute-start.1 = (bf16[8,128,512]{2,1,0:T(8,128)(2,1)}, bf16[8,128,512]{2,1,0:T(8,128)(2,1)}, u32[]{:S(2)}, u32[]{:S(2)}) collective-permute-start(bf16[8,128,512]{2,1,0:T(8,128)(2,1)} %slice.64.refs_0_), channel_id=1, source_target_pairs={{0,2},{1,3},{2,0},{3,1},{4,6},{5,7},{6,4},{7,5},{8,10},{9,11},{10,... | collective-permute-start | bytes 3145736 | tf_op jit(solution)/shard_map/ppermute | solution.py:337
  110.6 4.1 %collective-permute-start.2 = (bf16[8,128,512]{2,1,0:T(8,128)(2,1)}, bf16[8,128,512]{2,1,0:T(8,128)(2,1)}, u32[]{:S(2)}, u32[]{:S(2)}) collective-permute-start(bf16[8,128,512]{2,1,0:T(8,128)(2,1)} %slice.64.refs_0_), channel_id=1, source_target_pairs={{0,3},{1,0},{2,1},{3,2},{4,7},{5,4},{6,5},{7,6},{8,11},{9,8},{10,9... | collective-permute-start | bytes 3145736 | tf_op jit(solution)/shard_map/ppermute | solution.py:337
  114.8 0.6 iota_bitcast_fusion
  115.4 0.6 multiply_reduce_fusion
  116.0 0.8 mul.110
  117.0 0.6 broadcast_add_fusion.1.t_ref
  117.7 0.7 broadcast_add_fusion.t_ref
  118.4 6.9 %all-to-all-done.1.d_ref = bf16[8,32,3072]{2,1,0:T(8,128)(2,1)S(1)} async-done(((bf16[8,32,3072]{2,1,0:T(8,128)(2,1)}), bf16[8,32,3072]{2,1,0:T(8,128)(2,1)S(1)}, u32[]{:S(2)}, u32[]{:S(2)}) %all-to-all-start.1) | async-done | bytes 1572896 | tf_op jit(solution)/shard_map/all_to_all | solution.py:352
  125.2 2.9 %convolution_convert_fusion.1 = bf16[256,1536]{1,0:T(8,128)(2,1)} fusion(pred[256,512]{1,0:T(32,128)(4,1)S(1)} %and.53, bf16[512,4608]{1,0:T(8,128)(2,1)} %all-gather.3.cloned.1.call-done), kind=kOutput, calls=%fused_computation.2 | convolution fusion | flops 403046400 | bytes 2490368 | tf_op jit(solution)/shard_map/dot_general | solution.py:356
  128.1 3.5 %all-to-all-start.2 = ((bf16[8,32,1536]{2,1,0:T(8,128)(2,1)}), bf16[8,32,1536]{2,1,0:T(8,128)(2,1)S(1)}, u32[]{:S(2)}, u32[]{:S(2)}) async-start(bf16[8,32,1536]{2,1,0:T(8,128)(2,1)} %bitcast.63), calls=%async_computation.2 | async-start | bytes 1572864 | tf_op jit(solution)/shard_map/all_to_all | solution.py:357
  131.7 0.7 collective-permute-done.refs_1_
  132.3 5.0 %collective-permute-done.1.refs_2_ = bf16[8,128,512]{2,1,0:T(8,128)(2,1)} collective-permute-done((bf16[8,128,512]{2,1,0:T(8,128)(2,1)}, bf16[8,128,512]{2,1,0:T(8,128)(2,1)}, u32[]{:S(2)}, u32[]{:S(2)}) %collective-permute-start.1) | collective-permute-done | bytes 1048608 | tf_op jit(solution)/shard_map/ppermute | solution.py:337
  137.3 21.7 %collective-permute-done.2.refs_3_ = bf16[8,128,512]{2,1,0:T(8,128)(2,1)} collective-permute-done((bf16[8,128,512]{2,1,0:T(8,128)(2,1)}, bf16[8,128,512]{2,1,0:T(8,128)(2,1)}, u32[]{:S(2)}, u32[]{:S(2)}) %collective-permute-start.2) | collective-permute-done | bytes 1048608 | tf_op jit(solution)/shard_map/ppermute | solution.py:337
  159.0 1.9 copy-done.1
  160.9 11.0 %shard_map.110 = bf16[2,512,192]{2,1,0:T(8,128)(2,1)S(1)} custom-call(s32[4]{0:T(128)S(1)} %pad_add_fusion.where_ref, bf16[2,2048,384]{2,1,0:T(8,128)(2,1)S(1)} %bitcast.59, bf16[8,32,3072]{2,1,0:T(8,128)(2,1)S(1)} %all-to-all-done.1.d_ref, s32[2,1,1024]{2,1,0:T(1,128)S(1)} %broadcast_add_fusion.t_ref, bf16[8,128,512]{2,1,0:T(8,128)(2,1)} %slice.64.refs_0_, ...), custom_call_target="tpu_custom_call" | custom-call | flops 4831838208 | bytes 10485760 | tf_op jit(solution)/shard_map/pallas_call | solution.py:132
  171.9 0.7 fusion.10
  172.8 13.4 %all_gather.18 = bf16[4,512,192]{1,2,0:T(8,128)(2,1)S(1)} all-gather(bf16[1,512,192]{1,2,0:T(8,128)(2,1)S(1)} %copy.79), channel_id=1, replica_groups=mesh['x'=4,'z'=16,'c'=2,'dp'=4] {'dp'}, dimensions={0}, use_global_device_ids=true | all-gather | bytes 983040 | tf_op jit(solution)/shard_map/all_gather | solution.py:367
  186.2 0.5 copy.84.h0_ref
  186.9 14.2 %all_gather.19 = bf16[4,512,192]{1,2,0:T(8,128)(2,1)} all-gather(bf16[1,512,192]{1,2,0:T(8,128)(2,1)S(1)} %copy.80), channel_id=1, replica_groups=mesh['x'=4,'z'=16,'c'=2,'dp'=4] {'dp'}, dimensions={0}, use_global_device_ids=true | all-gather | bytes 983040 | tf_op jit(solution)/shard_map/all_gather | solution.py:368
  201.1 1.4 copy.85.h1_ref
  202.6 1.4 copy-done
  204.0 1.2 shard_map.111.w_ref
  205.2 2.2 shard_map.112
  207.4 4.4 %all-to-all-start.3 = ((bf16[8,128,512]{2,1,0:T(8,128)(2,1)}), bf16[8,128,512]{2,1,0:T(8,128)(2,1)S(1)}, u32[]{:S(2)}, u32[]{:S(2)}) async-start(bf16[8,128,512]{2,1,0:T(8,128)(2,1)} %bitcast.26), calls=%async_computation.3 | async-start | bytes 2097152 | tf_op jit(solution)/shard_map/all_to_all | solution.py:371
  211.9 0.1 convert_element_type.103.target_ref
  212.0 15.8 %all-to-all-done.3 = bf16[8,128,512]{2,1,0:T(8,128)(2,1)S(1)} async-done(((bf16[8,128,512]{2,1,0:T(8,128)(2,1)}), bf16[8,128,512]{2,1,0:T(8,128)(2,1)S(1)}, u32[]{:S(2)}, u32[]{:S(2)}) %all-to-all-start.3) | async-done | bytes 1048608 | tf_op jit(solution)/shard_map/all_to_all | solution.py:371
  227.8 2.1 shard_map.113
  229.9 35.6 %all_to_all.25 = bf16[16,32,512]{2,1,0:T(8,128)(2,1)S(1)} all-to-all(bf16[16,32,512]{2,1,0:T(8,128)(2,1)S(1)} %shard_map.113), channel_id=1, replica_groups=mesh['x'=4,'z'=16,'c'=2,'dp'=4] {'z'}, dimensions={0} | all-to-all | bytes 1048576 | tf_op jit(solution)/shard_map/all_to_all | solution.py:374
  265.5 0.7 reduce_sum.52
  (66 shorter events, 2.5 us)
Async XLA Ops:
  6.5 2.9 %copy-start.4 = (s32[2,16,8]{1,2,0:T(8,128)S(1)}, s32[2,16,8]{1,2,0:T(8,128)}, u32[]{:S(2)}) copy-start(s32[2,16,8]{1,2,0:T(8,128)} %param.12) | copy-start | bytes 3076
  6.5 3.0 %copy-start.6 = (s32[128,2]{0,1:T(2,128)S(1)}, s32[128,2]{0,1:T(2,128)}, u32[]{:S(2)}) copy-start(s32[128,2]{0,1:T(2,128)} %param.15) | copy-start | bytes 3076
  6.5 3.3 %copy-start.7 = (s32[2,1,128]{2,1,0:T(1,128)S(1)}, s32[2,1,128]{2,1,0:T(1,128)}, u32[]{:S(2)}) copy-start(s32[2,1,128]{2,1,0:T(1,128)} %param.14) | copy-start | bytes 3076
  6.5 3.8 %copy-start.5 = (f32[2,16,8]{1,2,0:T(8,128)S(1)}, f32[2,16,8]{1,2,0:T(8,128)}, u32[]{:S(2)}) copy-start(f32[2,16,8]{1,2,0:T(8,128)} %param.13) | copy-start | bytes 3076
  6.5 3.9 %copy-start.9 = (s32[1,32]{1,0:T(1,128)S(1)}, s32[1,32]{1,0:T(1,128)}, u32[]{:S(2)}) copy-start(s32[1,32]{1,0:T(1,128)} %param.18) | copy-start | bytes 388
  6.5 3.9 %copy-start.8 = (s32[1,32]{1,0:T(1,128)S(1)}, s32[1,32]{1,0:T(1,128)}, u32[]{:S(2)}) copy-start(s32[1,32]{1,0:T(1,128)} %param.19) | copy-start | bytes 388
  6.6 4.2 %copy-start.3 = (bf16[2,16,512]{2,1,0:T(8,128)(2,1)S(1)}, bf16[2,16,512]{2,1,0:T(8,128)(2,1)}, u32[]{:S(2)}) copy-start(bf16[2,16,512]{2,1,0:T(8,128)(2,1)} %param.11) | copy-start | bytes 98308
  6.6 88.3 %all-gather.3.cloned.1.call-start = ((), (), s32[]{:S(2)}) async-start(), calls=%async_computation.5 | async-start | bytes 5013504 | tf_op jit(solution)/shard_map/all_gather | solution.py:279
  56.8 21.9 %all-to-all-start = ((bf16[8,144,512]{2,1,0:T(8,128)(2,1)}), bf16[8,144,512]{2,1,0:T(8,128)(2,1)S(1)}, u32[]{:S(2)}, u32[]{:S(2)}) async-start(bf16[8,144,512]{2,1,0:T(8,128)(2,1)} %shard_map.109), calls=%async_computation | async-start | bytes 2359296 | tf_op jit(solution)/shard_map/all_to_all | solution.py:334
  99.0 26.3 %all-to-all-start.1 = ((bf16[8,32,3072]{2,1,0:T(8,128)(2,1)}), bf16[8,32,3072]{2,1,0:T(8,128)(2,1)S(1)}, u32[]{:S(2)}, u32[]{:S(2)}) async-start(bf16[8,32,3072]{2,1,0:T(8,128)(2,1)} %bitcast.62), calls=%async_computation.1 | async-start | bytes 3145728 | tf_op jit(solution)/shard_map/all_to_all | solution.py:352
  104.2 28.2 %collective-permute-start = (bf16[8,128,512]{2,1,0:T(8,128)(2,1)}, bf16[8,128,512]{2,1,0:T(8,128)(2,1)}, u32[]{:S(2)}, u32[]{:S(2)}) collective-permute-start(bf16[8,128,512]{2,1,0:T(8,128)(2,1)} %slice.64.refs_0_), channel_id=1, source_target_pairs={{0,1},{1,2},{2,3},{3,0},{4,5},{5,6},{6,7},{7,4},{8,9},{9,10},{10,1... | collective-permute-start | bytes 3145736 | tf_op jit(solution)/shard_map/ppermute | solution.py:337
  107.5 29.8 %collective-permute-start.1 = (bf16[8,128,512]{2,1,0:T(8,128)(2,1)}, bf16[8,128,512]{2,1,0:T(8,128)(2,1)}, u32[]{:S(2)}, u32[]{:S(2)}) collective-permute-start(bf16[8,128,512]{2,1,0:T(8,128)(2,1)} %slice.64.refs_0_), channel_id=1, source_target_pairs={{0,2},{1,3},{2,0},{3,1},{4,6},{5,7},{6,4},{7,5},{8,10},{9,11},{10,... | collective-permute-start | bytes 3145736 | tf_op jit(solution)/shard_map/ppermute | solution.py:337
  110.6 48.4 %collective-permute-start.2 = (bf16[8,128,512]{2,1,0:T(8,128)(2,1)}, bf16[8,128,512]{2,1,0:T(8,128)(2,1)}, u32[]{:S(2)}, u32[]{:S(2)}) collective-permute-start(bf16[8,128,512]{2,1,0:T(8,128)(2,1)} %slice.64.refs_0_), channel_id=1, source_target_pairs={{0,3},{1,0},{2,1},{3,2},{4,7},{5,4},{6,5},{7,6},{8,11},{9,8},{10,9... | collective-permute-start | bytes 3145736 | tf_op jit(solution)/shard_map/ppermute | solution.py:337
  128.1 74.4 %all-to-all-start.2 = ((bf16[8,32,1536]{2,1,0:T(8,128)(2,1)}), bf16[8,32,1536]{2,1,0:T(8,128)(2,1)S(1)}, u32[]{:S(2)}, u32[]{:S(2)}) async-start(bf16[8,32,1536]{2,1,0:T(8,128)(2,1)} %bitcast.63), calls=%async_computation.2 | async-start | bytes 1572864 | tf_op jit(solution)/shard_map/all_to_all | solution.py:357
  159.0 1.9 copy-start.1
  172.7 14.1 %copy-start.2 = (bf16[1,512,192]{2,1,0:T(8,128)(2,1)S(1)}, bf16[1,512,192]{2,1,0:T(8,128)(2,1)}, u32[]{:S(2)}) copy-start(bf16[1,512,192]{2,1,0:T(8,128)(2,1)} %get-tuple-element.17) | copy-start | bytes 589828
  202.6 1.4 copy-start
  207.4 20.4 %all-to-all-start.3 = ((bf16[8,128,512]{2,1,0:T(8,128)(2,1)}), bf16[8,128,512]{2,1,0:T(8,128)(2,1)S(1)}, u32[]{:S(2)}, u32[]{:S(2)}) async-start(bf16[8,128,512]{2,1,0:T(8,128)(2,1)} %bitcast.26), calls=%async_computation.3 | async-start | bytes 2097152 | tf_op jit(solution)/shard_map/all_to_all | solution.py:371
Sparse Core Ops, SparseCore 0:
  9.5 85.3 all-gather.2

commit v2 on v1

--- a/solution.py
+++ b/solution.py
@@ -108,7 +108,7 @@
     half = cols // 2
     up = pltpu.roll(acc, half, 1)
     act = acc / (1.0 + jnp.exp(-acc)) * up
-    out_ref[0] = act[:, :half].astype(BF)
+    out_ref[0] = act.T[:half].astype(BF)
 
 
 def gate_hidden(where, gate_up, deltas, targets, toks, br):
@@ -126,13 +126,13 @@
             pl.BlockSpec((1, 1, br * learners), lambda j, w: (j, 0, 0)),
         ]
         + [pl.BlockSpec((peers, rows // 2, quarter), lambda j, w: (0, j, 0))] * len(toks),
-        out_specs=pl.BlockSpec((1, slot_rows, cols // 2), lambda j, w: (j, 0, 0)),
+        out_specs=pl.BlockSpec((1, cols // 2, slot_rows), lambda j, w: (j, 0, 0)),
         scratch_shapes=[pltpu.VMEM((br * learners, cols), BF)],
     )
     return pl.pallas_call(
         functools.partial(gate_kernel, br),
         grid_spec=grid_spec,
-        out_shape=jax.ShapeDtypeStruct((2, slot_rows, cols // 2), BF),
+        out_shape=jax.ShapeDtypeStruct((2, cols // 2, slot_rows), BF),
         compiler_params=PARAMS,
         cost_estimate=pl.CostEstimate(
             flops=4 * depth * cols * (slot_rows + br * learners),
@@ -181,20 +181,23 @@
 
 
 def out_kernel(peers, h0_ref, h1_ref, w_ref, out_ref):
-    parts, slot_rows, hd = h0_ref.shape
+    parts, hd, slot_rows = h0_ref.shape
     cols = w_ref.shape[2]
     for j, h_ref in enumerate((h0_ref, h1_ref)):
         acc = None
         for p in range(parts):
-            term = jnp.dot(
-                h_ref[p], w_ref[j, p * hd : (p + 1) * hd, :], preferred_element_type=F32
+            term = lax.dot_general(
+                h_ref[p],
+                w_ref[j, p * hd : (p + 1) * hd, :],
+                (((0,), (0,)), ((), ())),
+                preferred_element_type=F32,
             )
             acc = term if acc is None else acc + term
         out_ref[:, j] = acc.astype(BF).reshape(peers, slot_rows // peers, cols)
 
 
 def expert_out(h0, h1, down, peers):
-    parts, slot_rows, hd = h0.shape
+    parts, hd, slot_rows = h0.shape
     cols = down.shape[2]
     return pl.pallas_call(
         functools.partial(out_kernel, peers),
@@ -347,7 +350,7 @@
     )
 
     cut = br * gate_cols
-    deltas, _ = lax.optimization_barrier((deltas, own))
+    deltas, *_ = lax.optimization_barrier((deltas, toks[1], toks[-1]))
     send_gate = jnp.dot(chosen, deltas[:, :cut], preferred_element_type=F32).astype(BF)
     got_gate = lax.all_to_all(
         send_gate.reshape(peers, 2 * nz, cut), XC, split_axis=0, concat_axis=0, tiled=True

time: 274 us -> 262 us (0.956)
  the two profiles are of different devices: /device:TPU:8 before, /device:TPU:2 now
where the time goes in v2:
time: 262 us; the launch traced here: 261 us
  blocking collectives  125 us (48%)
  waiting for transfers between devices  54.8 us (21%)
  starting transfers between devices  24.6 us (9%)
  Pallas kernels  17.4 us (7%)
  between operations  13.7 us (5%)
  local copies, waits for them, and re-layouts  12.6 us (5%)
  matrix products  7.35 us (3%)
  other arithmetic  5.86 us (2%)
    all_gather x1, blocking collectives, on_device(): packets = lax.all_gather(packet, 'z', axis=0, tiled=False)  42.2 us
    all_to_all x1, blocking collectives, on_device(): lax.all_to_all(partial, 'z', split_axis=0, concat_axis=0, tiled=True)  33.4 us
    ppermute x3, waiting for transfers between devices, on_device(): lax.ppermute(own, 'dp', [(i, (i + n) % nd) for i in range(nd)])  23.4 us
    all_to_all x1, blocking collectives, on_device(): got = lax.all_to_all(picked, XC, split_axis=0, concat_axis=0, tiled=True)  20.7 us
    all_to_all x1, waiting for transfers between devices, on_device(): lax.all_to_all(send_gate.reshape(peers, 2 * nz, cut), XC, split_axis=0, c...  17 us
    all_gather x1, blocking collectives, on_device(): h0 = lax.all_gather(hidden[0], 'dp', axis=0, tiled=False)  14.5 us
    all_to_all x1, waiting for transfers between devices, on_device(): back = lax.all_to_all(out, XC, split_axis=0, concat_axis=0, tiled=True)  14.4 us
    all_gather x1, blocking collectives, on_device(): h1 = lax.all_gather(hidden[1], 'dp', axis=0, tiled=False)  14 us
  transfers between devices with their start and end apart: 7, of which 5 were waited for; matrix products, arithmetic and copies ran while one was open for 4% of the time, Pallas kernels for 5%

profile of v2, /device:TPU:2, one launch (start us, length us, event | category | flops | bytes accessed | tf_op | source)
XLA Modules:
  0.0 261.2 jit_solution(1851427638477320795)
XLA Ops:
  6.6 1.0 copy.65
  7.7 1.0 copy.75
  8.6 0.7 pad_maximum_fusion
  9.6 0.1 copy.64
  9.8 0.1 eq.88
  9.9 0.1 reshape.306
  10.0 0.1 select_reduce_fusion.2
  10.2 0.2 select_reduce_fusion.1
  10.4 0.1 convert_element_type.92
  10.7 0.1 copy.74
  11.0 0.1 convert_element_type.104.target_ref
  11.2 42.2 %all-gather = bf16[512,640]{1,0:T(8,128)(2,1)S(1)} all-gather(bf16[32,640]{1,0:T(8,128)(2,1)S(1)} %pad_maximum_fusion.1), channel_id=2, replica_groups=mesh['x'=4,'z'=16,'c'=2,'dp'=4] {'z'}, dimensions={0}, use_global_device_ids=true | all-gather | bytes 696320 | tf_op jit(solution)/shard_map/all_gather | solution.py:295
  53.4 0.4 fusion.2
  53.8 0.2 select_reduce_fusion
  54.1 1.0 slice_add_fusion
  55.1 0.1 copy.68.code_ref
  55.3 1.0 shard_map.109
  56.3 20.7 %all_to_all.25 = bf16[8,144,512]{2,1,0:T(8,128)(2,1)S(1)} all-to-all(bf16[8,144,512]{2,1,0:T(8,128)(2,1)S(1)} %shard_map.109), channel_id=1, replica_groups=mesh['x'=4,'z'=16,'c'=2,'dp'=4] {'x','c'}, dimensions={0} | all-to-all | bytes 2359296 | tf_op jit(solution)/shard_map/all_to_all | solution.py:337
  77.1 1.0 copy-done.8
  78.1 6.3 %collective-permute-start.1 = (bf16[8,128,512]{2,1,0:T(8,128)(2,1)S(1)}, bf16[8,128,512]{2,1,0:T(8,128)(2,1)S(1)}, u32[]{:S(2)}, u32[]{:S(2)}) collective-permute-start(bf16[8,128,512]{2,1,0:T(8,128)(2,1)S(1)} %slice.64.refs_0_), channel_id=1, source_target_pairs={{0,3},{1,0},{2,1},{3,2},{4,7},{5,4},{6,5},{7,6},{8,11},{9,8},{10,9... | collective-permute-start | bytes 3145736 | tf_op jit(solution)/shard_map/ppermute | solution.py:340
  84.4 1.9 collective-permute-start
  86.4 1.2 broadcast_and_fusion
  87.6 2.1 and.53
  89.7 17.3 %collective-permute-done.1.refs_3_ = bf16[8,128,512]{2,1,0:T(8,128)(2,1)S(1)} collective-permute-done((bf16[8,128,512]{2,1,0:T(8,128)(2,1)S(1)}, bf16[8,128,512]{2,1,0:T(8,128)(2,1)S(1)}, u32[]{:S(2)}, u32[]{:S(2)}) %collective-permute-start.1) | collective-permute-done | bytes 1048608 | tf_op jit(solution)/shard_map/ppermute | solution.py:340
  107.0 5.3 %collective-permute-done.refs_1_ = bf16[8,128,512]{2,1,0:T(8,128)(2,1)S(1)} collective-permute-done((bf16[8,128,512]{2,1,0:T(8,128)(2,1)S(1)}, bf16[8,128,512]{2,1,0:T(8,128)(2,1)S(1)}, u32[]{:S(2)}, u32[]{:S(2)}) %collective-permute-start) | collective-permute-done | bytes 1048608 | tf_op jit(solution)/shard_map/ppermute | solution.py:340
  112.3 4.4 %convolution_convert_fusion = bf16[256,3072]{1,0:T(8,128)(2,1)} fusion(pred[256,512]{1,0:T(32,128)(4,1)S(1)} %and.53, bf16[512,4608]{1,0:T(8,128)(2,1)} %all-gather.3.cloned.1.call-done), kind=kOutput, calls=%fused_computation | convolution fusion | flops 806092800 | bytes 4849664 | tf_op jit(solution)/shard_map/dot_general | solution.py:354
  116.8 4.6 %all-to-all-start.1 = ((bf16[8,32,3072]{2,1,0:T(8,128)(2,1)}), bf16[8,32,3072]{2,1,0:T(8,128)(2,1)S(1)}, u32[]{:S(2)}, u32[]{:S(2)}) async-start(bf16[8,32,3072]{2,1,0:T(8,128)(2,1)} %bitcast.62), calls=%async_computation.1 | async-start | bytes 3145728 | tf_op jit(solution)/shard_map/all_to_all | solution.py:355
  121.4 1.9 collective-permute-start.2
  123.4 0.7 multiply_reduce_fusion
  124.5 17.0 %all-to-all-done.1.d_ref = bf16[8,32,3072]{2,1,0:T(8,128)(2,1)S(1)} async-done(((bf16[8,32,3072]{2,1,0:T(8,128)(2,1)}), bf16[8,32,3072]{2,1,0:T(8,128)(2,1)S(1)}, u32[]{:S(2)}, u32[]{:S(2)}) %all-to-all-start.1) | async-done | bytes 1572896 | tf_op jit(solution)/shard_map/all_to_all | solution.py:355
  141.5 2.9 %convolution_convert_fusion.1 = bf16[256,1536]{1,0:T(8,128)(2,1)} fusion(pred[256,512]{1,0:T(32,128)(4,1)S(1)} %and.53, bf16[512,4608]{1,0:T(8,128)(2,1)} %all-gather.3.cloned.1.call-done), kind=kOutput, calls=%fused_computation.2 | convolution fusion | flops 403046400 | bytes 2490368 | tf_op jit(solution)/shard_map/dot_general | solution.py:359
  144.4 4.9 %all-to-all-start.2 = ((bf16[8,32,1536]{2,1,0:T(8,128)(2,1)}), bf16[8,32,1536]{2,1,0:T(8,128)(2,1)S(1)}, u32[]{:S(2)}, u32[]{:S(2)}) async-start(bf16[8,32,1536]{2,1,0:T(8,128)(2,1)} %bitcast.63), calls=%async_computation.2 | async-start | bytes 1572864 | tf_op jit(solution)/shard_map/all_to_all | solution.py:360
  149.3 0.7 collective-permute-done.2.refs_2_
  150.1 1.9 copy-done.3
  152.0 1.2 copy-done.5
  153.2 1.2 copy-done.7
  154.4 10.8 %shard_map.110 = bf16[2,192,512]{2,1,0:T(8,128)(2,1)S(1)} custom-call(s32[4]{0:T(128)S(1)} %pad_add_fusion.where_ref, bf16[2,2048,384]{2,1,0:T(8,128)(2,1)S(1)} %bitcast.59, bf16[8,32,3072]{2,1,0:T(8,128)(2,1)S(1)} %all-to-all-done.1.d_ref, s32[2,1,1024]{2,1,0:T(1,128)S(1)} %broadcast_add_fusion.t_ref, bf16[8,128,512]{2,1,0:T(8,128)(2,1)S(1)} %slice.64.refs_0_, ...), custom_call_target="tpu_custom_call" | custom-call | flops 4831838208 | bytes 10485760 | tf_op jit(solution)/shard_map/pallas_call | solution.py:132
  165.3 14.0 %all_gather.19.h1_ref = bf16[4,192,512]{2,1,0:T(8,128)(2,1)S(1)} all-gather(bf16[1,192,512]{2,1,0:T(8,128)(2,1)S(1)} %get-tuple-element.17), channel_id=1, replica_groups=mesh['x'=4,'z'=16,'c'=2,'dp'=4] {'dp'}, dimensions={0}, use_global_device_ids=true | all-gather | bytes 983040 | tf_op jit(solution)/shard_map/all_gather | solution.py:371
  179.3 14.5 %all_gather.18.h0_ref = bf16[4,192,512]{2,1,0:T(8,128)(2,1)S(1)} all-gather(bf16[1,192,512]{2,1,0:T(8,128)(2,1)S(1)} %get-tuple-element.18), channel_id=1, replica_groups=mesh['x'=4,'z'=16,'c'=2,'dp'=4] {'dp'}, dimensions={0}, use_global_device_ids=true | all-gather | bytes 983040 | tf_op jit(solution)/shard_map/all_gather | solution.py:370
  193.8 1.4 copy-done
  195.2 1.2 shard_map.111.w_ref
  196.4 2.3 shard_map.112
  198.7 5.0 %all-to-all-start.3 = ((bf16[8,128,512]{2,1,0:T(8,128)(2,1)}), bf16[8,128,512]{2,1,0:T(8,128)(2,1)S(1)}, u32[]{:S(2)}, u32[]{:S(2)}) async-start(bf16[8,128,512]{2,1,0:T(8,128)(2,1)} %bitcast.26), calls=%async_computation.3 | async-start | bytes 2097152 | tf_op jit(solution)/shard_map/all_to_all | solution.py:374
  203.7 0.1 convert_element_type.103.target_ref
  203.8 14.4 %all-to-all-done.3 = bf16[8,128,512]{2,1,0:T(8,128)(2,1)S(1)} async-done(((bf16[8,128,512]{2,1,0:T(8,128)(2,1)}), bf16[8,128,512]{2,1,0:T(8,128)(2,1)S(1)}, u32[]{:S(2)}, u32[]{:S(2)}) %all-to-all-start.3) | async-done | bytes 1048608 | tf_op jit(solution)/shard_map/all_to_all | solution.py:374
  218.2 2.1 shard_map.113
  220.2 33.4 %all_to_all.26 = bf16[16,32,512]{2,1,0:T(8,128)(2,1)S(1)} all-to-all(bf16[16,32,512]{2,1,0:T(8,128)(2,1)S(1)} %shard_map.113), channel_id=1, replica_groups=mesh['x'=4,'z'=16,'c'=2,'dp'=4] {'z'}, dimensions={0} | all-to-all | bytes 1048576 | tf_op jit(solution)/shard_map/all_to_all | solution.py:377
  253.7 0.7 reduce_sum.52
  (73 shorter events, 1.7 us)
Async XLA Ops:
  6.5 3.0 %copy-start.14 = (s32[1,32]{1,0:T(1,128)S(1)}, s32[1,32]{1,0:T(1,128)}, u32[]{:S(2)}) copy-start(s32[1,32]{1,0:T(1,128)} %param.19) | copy-start | bytes 388
  6.5 3.0 %copy-start.15 = (s32[1,32]{1,0:T(1,128)S(1)}, s32[1,32]{1,0:T(1,128)}, u32[]{:S(2)}) copy-start(s32[1,32]{1,0:T(1,128)} %param.18) | copy-start | bytes 388
  6.5 3.1 %copy-start.10 = (s32[2,16,8]{1,2,0:T(8,128)S(1)}, s32[2,16,8]{1,2,0:T(8,128)}, u32[]{:S(2)}) copy-start(s32[2,16,8]{1,2,0:T(8,128)} %param.12) | copy-start | bytes 3076
  6.5 3.3 %copy-start.12 = (s32[128,2]{0,1:T(2,128)S(1)}, s32[128,2]{0,1:T(2,128)}, u32[]{:S(2)}) copy-start(s32[128,2]{0,1:T(2,128)} %param.15) | copy-start | bytes 3076
  6.5 3.6 %copy-start.13 = (s32[2,1,128]{2,1,0:T(1,128)S(1)}, s32[2,1,128]{2,1,0:T(1,128)}, u32[]{:S(2)}) copy-start(s32[2,1,128]{2,1,0:T(1,128)} %param.14) | copy-start | bytes 3076
  6.5 4.0 %copy-start.11 = (f32[2,16,8]{1,2,0:T(8,128)S(1)}, f32[2,16,8]{1,2,0:T(8,128)}, u32[]{:S(2)}) copy-start(f32[2,16,8]{1,2,0:T(8,128)} %param.13) | copy-start | bytes 3076
  6.6 4.6 %copy-start.9 = (bf16[2,16,512]{2,1,0:T(8,128)(2,1)S(1)}, bf16[2,16,512]{2,1,0:T(8,128)(2,1)}, u32[]{:S(2)}) copy-start(bf16[2,16,512]{2,1,0:T(8,128)(2,1)} %param.11) | copy-start | bytes 98308
  6.6 105.8 %all-gather.3.cloned.1.call-start = ((), (), s32[]{:S(2)}) async-start(), calls=%async_computation.5 | async-start | bytes 5013504 | tf_op jit(solution)/shard_map/all_gather | solution.py:282
  77.0 1.0 copy-start.8
  78.1 28.9 %collective-permute-start.1 = (bf16[8,128,512]{2,1,0:T(8,128)(2,1)S(1)}, bf16[8,128,512]{2,1,0:T(8,128)(2,1)S(1)}, u32[]{:S(2)}, u32[]{:S(2)}) collective-permute-start(bf16[8,128,512]{2,1,0:T(8,128)(2,1)S(1)} %slice.64.refs_0_), channel_id=1, source_target_pairs={{0,3},{1,0},{2,1},{3,2},{4,7},{5,4},{6,5},{7,6},{8,11},{9,8},{10,9... | collective-permute-start | bytes 3145736 | tf_op jit(solution)/shard_map/ppermute | solution.py:340
  84.4 27.9 %collective-permute-start = (bf16[8,128,512]{2,1,0:T(8,128)(2,1)S(1)}, bf16[8,128,512]{2,1,0:T(8,128)(2,1)S(1)}, u32[]{:S(2)}, u32[]{:S(2)}) collective-permute-start(bf16[8,128,512]{2,1,0:T(8,128)(2,1)S(1)} %slice.64.refs_0_), channel_id=1, source_target_pairs={{0,1},{1,2},{2,3},{3,0},{4,5},{5,6},{6,7},{7,4},{8,9},{9,10},{10,1... | collective-permute-start | bytes 3145736 | tf_op jit(solution)/shard_map/ppermute | solution.py:340
  107.0 9.8 %copy-start.4 = (bf16[8,128,512]{2,1,0:T(8,128)(2,1)}, bf16[8,128,512]{2,1,0:T(8,128)(2,1)S(1)}, u32[]{:S(2)}) copy-start(bf16[8,128,512]{2,1,0:T(8,128)(2,1)S(1)} %collective-permute-done.1.refs_3_) | copy-start | bytes 3145732
  112.3 4.4 %copy-start.6 = (bf16[8,128,512]{2,1,0:T(8,128)(2,1)}, bf16[8,128,512]{2,1,0:T(8,128)(2,1)S(1)}, u32[]{:S(2)}) copy-start(bf16[8,128,512]{2,1,0:T(8,128)(2,1)S(1)} %collective-permute-done.refs_1_) | copy-start | bytes 3145732
  116.8 24.8 %all-to-all-start.1 = ((bf16[8,32,3072]{2,1,0:T(8,128)(2,1)}), bf16[8,32,3072]{2,1,0:T(8,128)(2,1)S(1)}, u32[]{:S(2)}, u32[]{:S(2)}) async-start(bf16[8,32,3072]{2,1,0:T(8,128)(2,1)} %bitcast.62), calls=%async_computation.1 | async-start | bytes 3145728 | tf_op jit(solution)/shard_map/all_to_all | solution.py:355
  121.4 28.7 %collective-permute-start.2 = (bf16[8,128,512]{2,1,0:T(8,128)(2,1)S(1)}, bf16[8,128,512]{2,1,0:T(8,128)(2,1)}, u32[]{:S(2)}, u32[]{:S(2)}) collective-permute-start(bf16[8,128,512]{2,1,0:T(8,128)(2,1)S(1)} %slice.64.refs_0_), channel_id=1, source_target_pairs={{0,2},{1,3},{2,0},{3,1},{4,6},{5,7},{6,4},{7,5},{8,10},{9,11},{10,... | collective-permute-start | bytes 3145736 | tf_op jit(solution)/shard_map/ppermute | solution.py:340
  144.4 49.3 %all-to-all-start.2 = ((bf16[8,32,1536]{2,1,0:T(8,128)(2,1)}), bf16[8,32,1536]{2,1,0:T(8,128)(2,1)S(1)}, u32[]{:S(2)}, u32[]{:S(2)}) async-start(bf16[8,32,1536]{2,1,0:T(8,128)(2,1)} %bitcast.63), calls=%async_computation.2 | async-start | bytes 1572864 | tf_op jit(solution)/shard_map/all_to_all | solution.py:360
  150.1 1.9 copy-start.3
  152.0 1.2 copy-start.5
  153.2 1.2 copy-start.7
  193.8 1.4 copy-start
  198.7 19.5 %copy-start.1 = (f32[2,256,8]{2,1,0:T(8,128)S(1)}, f32[2,256,8]{2,1,0:T(8,128)}, u32[]{:S(2)}) copy-start(f32[2,256,8]{2,1,0:T(8,128)} %get-tuple-element.19.gate_ref) | copy-start | bytes 49156
  198.7 19.5 %copy-start.2 = (f32[2,256,8]{2,1,0:T(8,128)S(1)}, f32[2,256,8]{2,1,0:T(8,128)}, u32[]{:S(2)}) copy-start(f32[2,256,8]{2,1,0:T(8,128)} %get-tuple-element.21.code_ref) | copy-start | bytes 49156
  198.7 19.5 %all-to-all-start.3 = ((bf16[8,128,512]{2,1,0:T(8,128)(2,1)}), bf16[8,128,512]{2,1,0:T(8,128)(2,1)S(1)}, u32[]{:S(2)}, u32[]{:S(2)}) async-start(bf16[8,128,512]{2,1,0:T(8,128)(2,1)} %bitcast.26), calls=%async_computation.3 | async-start | bytes 2097152 | tf_op jit(solution)/shard_map/all_to_all | solution.py:374
Sparse Core Ops, SparseCore 0:
  9.5 86.2 all-gather.2

commit v3 on v2

--- a/solution.py
+++ b/solution.py
@@ -80,8 +80,10 @@
     )(packets, codes_t, target_col, labels)
 
 
-def gate_kernel(br, where_ref, w_ref, d_ref, t_ref, *refs):
+def gate_kernel(br, last, where_ref, w_ref, d_ref, t_ref, *refs):
     tok_refs, out_ref, cat_ref = refs[:-2], refs[-2], refs[-1]
+    if last:
+        tok_refs, sum_ref = tok_refs[:-1], tok_refs[-1]
     peers, zs, _ = d_ref.shape
     depth, cols = w_ref.shape[1:]
     learners = peers * zs
@@ -94,7 +96,7 @@
     chunk = min(256, quarter)
     row_ids = lax.broadcasted_iota(jnp.int32, (chunk, br * learners), 0)
     tgt = t_ref[0]
-    acc = None
+    acc = sum_ref[0] if last else None
     for n in range(parts):
         q = where_ref[n]
         for c in range(quarter // chunk):
@@ -105,18 +107,24 @@
             toks = tok_refs[n][:, :, c * chunk : (c + 1) * chunk].reshape(-1, chunk)
             term = jnp.dot(toks, fresh, preferred_element_type=F32)
             acc = term if acc is None else acc + term
+    if not last:
+        out_ref[0] = acc
+        return
     half = cols // 2
     up = pltpu.roll(acc, half, 1)
     act = acc / (1.0 + jnp.exp(-acc)) * up
     out_ref[0] = act.T[:half].astype(BF)
 
 
-def gate_hidden(where, gate_up, deltas, targets, toks, br):
+def gate_hidden(where, gate_up, deltas, targets, toks, br, sums=None):
+    last = sums is not None
     _, depth, cols = gate_up.shape
     peers, rows, quarter = toks[0].shape
     zs = deltas.shape[1] // 2
     slot_rows = peers * rows // 2
     learners = peers * zs
+    shape = (cols // 2, slot_rows) if last else (slot_rows, cols)
+    sum_specs = [pl.BlockSpec((1, slot_rows, cols), lambda j, w: (j, 0, 0))] if last else []
     grid_spec = pltpu.PrefetchScalarGridSpec(
         num_scalar_prefetch=1,
         grid=(2,),
@@ -125,21 +133,22 @@
             pl.BlockSpec((peers, zs, deltas.shape[2]), lambda j, w: (0, j, 0)),
             pl.BlockSpec((1, 1, br * learners), lambda j, w: (j, 0, 0)),
         ]
-        + [pl.BlockSpec((peers, rows // 2, quarter), lambda j, w: (0, j, 0))] * len(toks),
-        out_specs=pl.BlockSpec((1, cols // 2, slot_rows), lambda j, w: (j, 0, 0)),
+        + [pl.BlockSpec((peers, rows // 2, quarter), lambda j, w: (0, j, 0))] * len(toks)
+        + sum_specs,
+        out_specs=pl.BlockSpec((1, *shape), lambda j, w: (j, 0, 0)),
         scratch_shapes=[pltpu.VMEM((br * learners, cols), BF)],
     )
     return pl.pallas_call(
-        functools.partial(gate_kernel, br),
+        functools.partial(gate_kernel, br, last),
         grid_spec=grid_spec,
-        out_shape=jax.ShapeDtypeStruct((2, cols // 2, slot_rows), BF),
+        out_shape=jax.ShapeDtypeStruct((2, *shape), BF if last else F32),
         compiler_params=PARAMS,
         cost_estimate=pl.CostEstimate(
-            flops=4 * depth * cols * (slot_rows + br * learners),
+            flops=len(toks) * depth * cols * (slot_rows + br * learners),
             bytes_accessed=10 * 1024 * 1024,
             transcendentals=2 * slot_rows * cols,
         ),
-    )(where, gate_up, deltas, targets, *toks)
+    )(where, gate_up, deltas, targets, *toks, *([sums] if last else []))
 
 
 def down_kernel(br, w_ref, d_ref, t_ref, out_ref, cat_ref):
@@ -339,7 +348,6 @@
     toks = [own] + [
         lax.ppermute(own, "dp", [(i, (i + n) % nd) for i in range(nd)]) for n in range(1, nd)
     ]
-    where = jnp.stack([(p - n) % nd for n in range(nd)]).astype(jnp.int32)
     block_of = got[:, count_rows, : 2 * nz].astype(F32).astype(jnp.int32) - 1
     block_of = block_of.reshape(peers, 2, nz).transpose(1, 0, 2).reshape(2, 1, peers * nz)
     gate_targets = (block_of * br + jnp.arange(br, dtype=jnp.int32)[None, :, None]).reshape(
@@ -350,13 +358,20 @@
     )
 
     cut = br * gate_cols
-    deltas, *_ = lax.optimization_barrier((deltas, toks[1], toks[-1]))
+    near = [0] + [n for n in range(1, nd) if n in (1, nd - 1)]
+    far = [n for n in range(1, nd) if n not in near]
+    where_near = jnp.stack([(p - n) % nd for n in near]).astype(jnp.int32)
+    where_far = jnp.stack([(p - n) % nd for n in far]).astype(jnp.int32)
     send_gate = jnp.dot(chosen, deltas[:, :cut], preferred_element_type=F32).astype(BF)
+    send_gate, *_ = lax.optimization_barrier((send_gate, toks[1], toks[-1]))
     got_gate = lax.all_to_all(
         send_gate.reshape(peers, 2 * nz, cut), XC, split_axis=0, concat_axis=0, tiled=True
     )
-    got_gate, deltas = lax.optimization_barrier((got_gate, deltas))
     send_down = jnp.dot(chosen, deltas[:, cut:], preferred_element_type=F32).astype(BF)
+    sums = gate_hidden(
+        where_near, gate_up[0], got_gate, gate_targets, [toks[n] for n in near], br
+    )
+    send_down, sums = lax.optimization_barrier((send_down, sums))
     got_down = lax.all_to_all(
         send_down.reshape(peers, 2 * nz, br2 * down_cols),
         XC,
@@ -364,8 +379,15 @@
         concat_axis=0,
         tiled=True,
     )
-
-    hidden = gate_hidden(where, gate_up[0], got_gate, gate_targets, toks, br)
+    hidden = gate_hidden(
+        where_far,
+        gate_up[0],
+        got_gate,
+        gate_targets,
+        [toks[n] for n in far],
+        br,
+        sums,
+    )
     down = fresh_down(down_proj[0], got_down, down_targets, br2)
     h0 = lax.all_gather(hidden[0], "dp", axis=0, tiled=False)
     h1 = lax.all_gather(hidden[1], "dp", axis=0, tiled=False)

time: 262 us -> 260 us (level)
  waiting for transfers between devices: 54.8 us -> 45.9 us
  local copies, waits for them, and re-layouts: 12.6 us -> 20.3 us
    ppermute x3, waiting for transfers between devices: 23.4 us -> 11.4 us  [on_device(): lax.ppermute(own, 'dp', [(i, (i + n) % nd) for i in range(nd)])]
    unnamed x36 -> x46, local copies, waits for them, and re-layouts: 8.8 us -> 16.5 us
    all_gather x1, waiting for transfers between devices: 0.01 us -> 5.96 us  [on_device(): deltas = lax.all_gather(flat_deltas, 'z', axis=0, tiled=True)]
    all_to_all x1, waiting for transfers between devices: 17 us -> 14.1 us  [on_device(): lax.all_to_all(send_gate.reshape(peers, 2 * nz, cut), XC, split_axis=0, c...]
    pallas_call x1 -> x2, Pallas kernels: 10.8 us -> 10.7 us  [gate_hidden(): pl.pallas_call(functools.partial(gate_kernel, br, last), grid_spec=grid_s...]
  transfers between devices with their start and end apart: 7 -> 7, of which waited for: 5 -> 5; matrix products, arithmetic and copies ran while one was open for 4% -> 6% of each run, Pallas kernels for 5% -> 4%
where the time goes in v3:
time: 260 us
  blocking collectives  125 us (48%)
  waiting for transfers between devices  45.9 us (18%)
  starting transfers between devices  24.9 us (10%)
  local copies, waits for them, and re-layouts  20.3 us (8%)
  Pallas kernels  17.2 us (7%)
  between operations  13.7 us (5%)
  matrix products  6.95 us (3%)
  other arithmetic  5.84 us (2%)
    all_gather x1, blocking collectives, on_device(): packets = lax.all_gather(packet, 'z', axis=0, tiled=False)  42.2 us
    all_to_all x1, blocking collectives, on_device(): lax.all_to_all(partial, 'z', split_axis=0, concat_axis=0, tiled=True)  33.4 us
    all_to_all x1, blocking collectives, on_device(): got = lax.all_to_all(picked, XC, split_axis=0, concat_axis=0, tiled=True)  20.7 us
    unnamed x46, local copies, waits for them, and re-layouts  16.5 us
    all_gather x1, blocking collectives, on_device(): h1 = lax.all_gather(hidden[1], 'dp', axis=0, tiled=False)  14.6 us
    all_to_all x1, waiting for transfers between devices, on_device(): back = lax.all_to_all(out, XC, split_axis=0, concat_axis=0, tiled=True)  14.4 us
    all_to_all x1, waiting for transfers between devices, on_device(): lax.all_to_all(send_gate.reshape(peers, 2 * nz, cut), XC, split_axis=0, c...  14.1 us
    all_gather x1, blocking collectives, on_device(): h0 = lax.all_gather(hidden[0], 'dp', axis=0, tiled=False)  13.7 us
  transfers between devices with their start and end apart: 7, of which 5 were waited for; matrix products, arithmetic and copies ran while one was open for 6% of the time, Pallas kernels for 4%

profile of v3, /device:TPU:2, one launch (start us, length us, event | category | flops | bytes accessed | tf_op | source)
XLA Modules:
  0.0 259.5 jit_solution(12950323162849208183)
XLA Ops:
  6.6 1.0 copy.65
  7.7 1.0 copy.75
  8.6 0.8 pad_maximum_fusion
  9.9 0.1 reshape.306
  10.2 0.2 select_reduce_fusion.1
  11.2 42.2 %all-gather = bf16[512,640]{1,0:T(8,128)(2,1)S(1)} all-gather(bf16[32,640]{1,0:T(8,128)(2,1)S(1)} %pad_maximum_fusion.1), channel_id=2, replica_groups=mesh['x'=4,'z'=16,'c'=2,'dp'=4] {'z'}, dimensions={0}, use_global_device_ids=true | all-gather | bytes 696320 | tf_op jit(solution)/shard_map/all_gather | solution.py:304
  53.4 0.4 fusion.2
  53.8 0.2 select_reduce_fusion
  54.1 1.0 slice_add_fusion
  55.2 1.0 shard_map.109
  56.3 20.7 %all_to_all.25 = bf16[8,144,512]{2,1,0:T(8,128)(2,1)S(1)} all-to-all(bf16[8,144,512]{2,1,0:T(8,128)(2,1)S(1)} %shard_map.109), channel_id=1, replica_groups=mesh['x'=4,'z'=16,'c'=2,'dp'=4] {'x','c'}, dimensions={0} | all-to-all | bytes 2359296 | tf_op jit(solution)/shard_map/all_to_all | solution.py:346
  77.1 0.9 copy-done.13
  78.0 6.3 %collective-permute-start.1 = (bf16[8,128,512]{2,1,0:T(8,128)(2,1)S(1)}, bf16[8,128,512]{2,1,0:T(8,128)(2,1)S(1)}, u32[]{:S(2)}, u32[]{:S(2)}) collective-permute-start(bf16[8,128,512]{2,1,0:T(8,128)(2,1)S(1)} %slice.65.refs_0_), channel_id=1, source_target_pairs={{0,3},{1,0},{2,1},{3,2},{4,7},{5,4},{6,5},{7,6},{8,11},{9,8},{10,9... | collective-permute-start | bytes 3145736 | tf_op jit(solution)/shard_map/ppermute | solution.py:349
  84.4 1.9 collective-permute-start
  86.4 1.2 broadcast_and_fusion
  87.5 2.1 and.50
  89.6 6.0 %all-gather.3.cloned.1.call-done = bf16[512,4608]{1,0:T(8,128)(2,1)} async-done(((bf16[32,4608]{1,0:T(8,128)(2,1)}), bf16[512,4608]{1,0:T(8,128)(2,1)}) %all-gather.3.cloned.1.call-update) | async-done | bytes 4718608 | tf_op jit(solution)/shard_map/all_gather | solution.py:291
  95.6 4.1 %convolution_convert_fusion = bf16[256,3072]{1,0:T(8,128)(2,1)} fusion(pred[256,512]{1,0:T(32,128)(4,1)S(1)} %and.50, bf16[512,4608]{1,0:T(8,128)(2,1)} %all-gather.3.cloned.1.call-done), kind=kOutput, calls=%fused_computation | convolution fusion | flops 806092800 | bytes 4849664 | tf_op jit(solution)/shard_map/dot_general | solution.py:365
  99.6 7.1 %collective-permute-done.1.refs_2_ = bf16[8,128,512]{2,1,0:T(8,128)(2,1)S(1)} collective-permute-done((bf16[8,128,512]{2,1,0:T(8,128)(2,1)S(1)}, bf16[8,128,512]{2,1,0:T(8,128)(2,1)S(1)}, u32[]{:S(2)}, u32[]{:S(2)}) %collective-permute-start.1) | collective-permute-done | bytes 1048608 | tf_op jit(solution)/shard_map/ppermute | solution.py:349
  106.7 1.0 copy-done.9
  107.7 4.3 %collective-permute-done.refs_1_ = bf16[8,128,512]{2,1,0:T(8,128)(2,1)S(1)} collective-permute-done((bf16[8,128,512]{2,1,0:T(8,128)(2,1)S(1)}, bf16[8,128,512]{2,1,0:T(8,128)(2,1)S(1)}, u32[]{:S(2)}, u32[]{:S(2)}) %collective-permute-start) | collective-permute-done | bytes 1048608 | tf_op jit(solution)/shard_map/ppermute | solution.py:349
  112.0 1.1 copy-done.11
  113.1 4.9 %all-to-all-start.1 = ((bf16[8,32,3072]{2,1,0:T(8,128)(2,1)}), bf16[8,32,3072]{2,1,0:T(8,128)(2,1)S(1)}, u32[]{:S(2)}, u32[]{:S(2)}) async-start(bf16[8,32,3072]{2,1,0:T(8,128)(2,1)} %bitcast.63), calls=%async_computation.1 | async-start | bytes 3145728 | tf_op jit(solution)/shard_map/all_to_all | solution.py:367
  118.0 1.9 collective-permute-start.2
  120.0 0.7 multiply_reduce_fusion
  121.1 2.9 %convolution_convert_fusion.1 = bf16[256,1536]{1,0:T(8,128)(2,1)} fusion(pred[256,512]{1,0:T(32,128)(4,1)S(1)} %and.50, bf16[512,4608]{1,0:T(8,128)(2,1)} %all-gather.3.cloned.1.call-done), kind=kOutput, calls=%fused_computation.2 | convolution fusion | flops 403046400 | bytes 2490368 | tf_op jit(solution)/shard_map/dot_general | solution.py:370
  124.0 14.1 %all-to-all-done.1.d_ref = bf16[8,32,3072]{2,1,0:T(8,128)(2,1)S(1)} async-done(((bf16[8,32,3072]{2,1,0:T(8,128)(2,1)}), bf16[8,32,3072]{2,1,0:T(8,128)(2,1)S(1)}, u32[]{:S(2)}, u32[]{:S(2)}) %all-to-all-start.1) | async-done | bytes 1572896 | tf_op jit(solution)/shard_map/all_to_all | solution.py:367
  138.1 1.9 copy-done
  140.0 1.2 copy-done.6
  141.2 1.2 copy-done.10
  142.5 1.2 copy-done.12
  143.7 7.4 %shard_map.110.refs_1_ = f32[2,512,384]{2,1,0:T(8,128)S(1)} custom-call(s32[3]{0:T(128)S(1)} %pad_add_fusion.where_ref, bf16[2,2048,384]{2,1,0:T(8,128)(2,1)S(1)} %bitcast.57, bf16[8,32,3072]{2,1,0:T(8,128)(2,1)S(1)} %all-to-all-done.1.d_ref, s32[2,1,1024]{2,1,0:T(1,128)S(1)} %broadcast_add_fusion.t_ref, bf16[8,128,512]{2,1,0:T(8,128)(2,1)S(1)} %copy-done.6, ...), custom_call_target="tpu_custom_call" | custom-call | flops 3623878656 | bytes 10485760 | tf_op jit(solution)/shard_map/pallas_call | solution.py:141
  151.1 1.2 copy-done.3
  152.2 4.9 %all-to-all-start.2 = ((bf16[8,32,1536]{2,1,0:T(8,128)(2,1)}), bf16[8,32,1536]{2,1,0:T(8,128)(2,1)S(1)}, u32[]{:S(2)}, u32[]{:S(2)}) async-start(bf16[8,32,1536]{2,1,0:T(8,128)(2,1)} %bitcast.64), calls=%async_computation.2 | async-start | bytes 1572864 | tf_op jit(solution)/shard_map/all_to_all | solution.py:375
  157.1 1.9 copy-done.1
  159.0 1.4 copy-done.4
  160.4 3.3 %shard_map.111 = bf16[2,192,512]{2,1,0:T(8,128)(2,1)S(1)} custom-call(s32[1]{0:T(128)} %bitcast.where_ref, bf16[2,2048,384]{2,1,0:T(8,128)(2,1)S(1)} %bitcast.58, bf16[8,32,3072]{2,1,0:T(8,128)(2,1)S(1)} %all-to-all-done.1.d_ref, s32[2,1,1024]{2,1,0:T(1,128)S(1)} %broadcast_add_fusion.t_ref, bf16[8,128,512]{2,1,0:T(8,128)(2,1)S(1)} %collective-permute-done.2.refs_0_, ...), custom_call_target="tpu_custom_call" | custom-call | flops 1207959552 | bytes 10485760 | tf_op jit(solution)/shard_map/pallas_call | solution.py:141
  163.8 14.6 %all_gather.19.h1_ref = bf16[4,192,512]{2,1,0:T(8,128)(2,1)S(1)} all-gather(bf16[1,192,512]{2,1,0:T(8,128)(2,1)S(1)} %get-tuple-element.17), channel_id=1, replica_groups=mesh['x'=4,'z'=16,'c'=2,'dp'=4] {'dp'}, dimensions={0}, use_global_device_ids=true | all-gather | bytes 983040 | tf_op jit(solution)/shard_map/all_gather | solution.py:393
  178.3 13.7 %all_gather.18.h0_ref = bf16[4,192,512]{2,1,0:T(8,128)(2,1)S(1)} all-gather(bf16[1,192,512]{2,1,0:T(8,128)(2,1)S(1)} %get-tuple-element.18), channel_id=1, replica_groups=mesh['x'=4,'z'=16,'c'=2,'dp'=4] {'dp'}, dimensions={0}, use_global_device_ids=true | all-gather | bytes 983040 | tf_op jit(solution)/shard_map/all_gather | solution.py:392
  192.1 1.4 copy-done.2
  193.5 1.2 shard_map.112.w_ref
  194.7 2.3 shard_map.113
  197.0 4.9 %all-to-all-start.3 = ((bf16[8,128,512]{2,1,0:T(8,128)(2,1)}), bf16[8,128,512]{2,1,0:T(8,128)(2,1)S(1)}, u32[]{:S(2)}, u32[]{:S(2)}) async-start(bf16[8,128,512]{2,1,0:T(8,128)(2,1)} %bitcast.26), calls=%async_computation.3 | async-start | bytes 2097152 | tf_op jit(solution)/shard_map/all_to_all | solution.py:396
  202.0 0.1 convert_element_type.103.target_ref
  202.1 14.4 %all-to-all-done.3 = bf16[8,128,512]{2,1,0:T(8,128)(2,1)S(1)} async-done(((bf16[8,128,512]{2,1,0:T(8,128)(2,1)}), bf16[8,128,512]{2,1,0:T(8,128)(2,1)S(1)}, u32[]{:S(2)}, u32[]{:S(2)}) %all-to-all-start.3) | async-done | bytes 1048608 | tf_op jit(solution)/shard_map/all_to_all | solution.py:396
  216.5 2.1 shard_map.114
  218.6 33.4 %all_to_all.26 = bf16[16,32,512]{2,1,0:T(8,128)(2,1)S(1)} all-to-all(bf16[16,32,512]{2,1,0:T(8,128)(2,1)S(1)} %shard_map.114), channel_id=1, replica_groups=mesh['x'=4,'z'=16,'c'=2,'dp'=4] {'z'}, dimensions={0} | all-to-all | bytes 1048576 | tf_op jit(solution)/shard_map/all_to_all | solution.py:399
  252.0 0.7 reduce_sum.52
  (84 shorter events, 2.4 us)
Async XLA Ops:
  6.5 3.0 %copy-start.19 = (s32[1,32]{1,0:T(1,128)S(1)}, s32[1,32]{1,0:T(1,128)}, u32[]{:S(2)}) copy-start(s32[1,32]{1,0:T(1,128)} %param.19) | copy-start | bytes 388
  6.5 3.0 %copy-start.20 = (s32[1,32]{1,0:T(1,128)S(1)}, s32[1,32]{1,0:T(1,128)}, u32[]{:S(2)}) copy-start(s32[1,32]{1,0:T(1,128)} %param.18) | copy-start | bytes 388
  6.5 3.2 %copy-start.15 = (s32[2,16,8]{1,2,0:T(8,128)S(1)}, s32[2,16,8]{1,2,0:T(8,128)}, u32[]{:S(2)}) copy-start(s32[2,16,8]{1,2,0:T(8,128)} %param.12) | copy-start | bytes 3076
  6.5 3.3 %copy-start.17 = (s32[128,2]{0,1:T(2,128)S(1)}, s32[128,2]{0,1:T(2,128)}, u32[]{:S(2)}) copy-start(s32[128,2]{0,1:T(2,128)} %param.15) | copy-start | bytes 3076
  6.5 3.6 %copy-start.18 = (s32[2,1,128]{2,1,0:T(1,128)S(1)}, s32[2,1,128]{2,1,0:T(1,128)}, u32[]{:S(2)}) copy-start(s32[2,1,128]{2,1,0:T(1,128)} %param.14) | copy-start | bytes 3076
  6.5 4.0 %copy-start.16 = (f32[2,16,8]{1,2,0:T(8,128)S(1)}, f32[2,16,8]{1,2,0:T(8,128)}, u32[]{:S(2)}) copy-start(f32[2,16,8]{1,2,0:T(8,128)} %param.13) | copy-start | bytes 3076
  6.6 4.6 %copy-start.14 = (bf16[2,16,512]{2,1,0:T(8,128)(2,1)S(1)}, bf16[2,16,512]{2,1,0:T(8,128)(2,1)}, u32[]{:S(2)}) copy-start(bf16[2,16,512]{2,1,0:T(8,128)(2,1)} %param.11) | copy-start | bytes 98308
  6.6 89.0 %all-gather.3.cloned.1.call-start = ((), (), s32[]{:S(2)}) async-start(), calls=%async_computation.5 | async-start | bytes 5013504 | tf_op jit(solution)/shard_map/all_gather | solution.py:291
  77.0 1.0 copy-start.13
  78.0 21.6 %copy-start.5 = (bf16[8,128,512]{2,1,0:T(8,128)(2,1)}, bf16[8,128,512]{2,1,0:T(8,128)(2,1)S(1)}, u32[]{:S(2)}) copy-start(bf16[8,128,512]{2,1,0:T(8,128)(2,1)S(1)} %slice.65.refs_0_) | copy-start | bytes 3145732
  78.0 28.7 %collective-permute-start.1 = (bf16[8,128,512]{2,1,0:T(8,128)(2,1)S(1)}, bf16[8,128,512]{2,1,0:T(8,128)(2,1)S(1)}, u32[]{:S(2)}, u32[]{:S(2)}) collective-permute-start(bf16[8,128,512]{2,1,0:T(8,128)(2,1)S(1)} %slice.65.refs_0_), channel_id=1, source_target_pairs={{0,3},{1,0},{2,1},{3,2},{4,7},{5,4},{6,5},{7,6},{8,11},{9,8},{10,9... | collective-permute-start | bytes 3145736 | tf_op jit(solution)/shard_map/ppermute | solution.py:349
  84.4 27.7 %collective-permute-start = (bf16[8,128,512]{2,1,0:T(8,128)(2,1)S(1)}, bf16[8,128,512]{2,1,0:T(8,128)(2,1)S(1)}, u32[]{:S(2)}, u32[]{:S(2)}) collective-permute-start(bf16[8,128,512]{2,1,0:T(8,128)(2,1)S(1)} %slice.65.refs_0_), channel_id=1, source_target_pairs={{0,1},{1,2},{2,3},{3,0},{4,5},{5,6},{6,7},{7,4},{8,9},{9,10},{10,1... | collective-permute-start | bytes 3145736 | tf_op jit(solution)/shard_map/ppermute | solution.py:349
  106.7 1.0 copy-start.9
  112.0 1.1 copy-start.11
  113.1 25.0 %all-to-all-start.1 = ((bf16[8,32,3072]{2,1,0:T(8,128)(2,1)}), bf16[8,32,3072]{2,1,0:T(8,128)(2,1)S(1)}, u32[]{:S(2)}, u32[]{:S(2)}) async-start(bf16[8,32,3072]{2,1,0:T(8,128)(2,1)} %bitcast.63), calls=%async_computation.1 | async-start | bytes 3145728 | tf_op jit(solution)/shard_map/all_to_all | solution.py:367
  118.0 39.1 %collective-permute-start.2 = (bf16[8,128,512]{2,1,0:T(8,128)(2,1)}, bf16[8,128,512]{2,1,0:T(8,128)(2,1)S(1)}, u32[]{:S(2)}, u32[]{:S(2)}) collective-permute-start(bf16[8,128,512]{2,1,0:T(8,128)(2,1)} %copy-done.5), channel_id=1, source_target_pairs={{0,2},{1,3},{2,0},{3,1},{4,6},{5,7},{6,4},{7,5},{8,10},{9,11},{10,... | collective-permute-start | bytes 3145736 | tf_op jit(solution)/shard_map/ppermute | solution.py:349
  138.1 1.9 copy-start
  140.0 1.2 copy-start.6
  141.2 1.2 copy-start.10
  142.5 1.2 copy-start.12
  151.1 1.2 copy-start.3
  152.2 39.9 %all-to-all-start.2 = ((bf16[8,32,1536]{2,1,0:T(8,128)(2,1)}), bf16[8,32,1536]{2,1,0:T(8,128)(2,1)S(1)}, u32[]{:S(2)}, u32[]{:S(2)}) async-start(bf16[8,32,1536]{2,1,0:T(8,128)(2,1)} %bitcast.64), calls=%async_computation.2 | async-start | bytes 1572864 | tf_op jit(solution)/shard_map/all_to_all | solution.py:375
  157.1 1.9 copy-start.1
  159.0 1.4 copy-start.4
  192.1 1.4 copy-start.2
  197.0 19.5 %copy-start.7 = (f32[2,256,8]{2,1,0:T(8,128)S(1)}, f32[2,256,8]{2,1,0:T(8,128)}, u32[]{:S(2)}) copy-start(f32[2,256,8]{2,1,0:T(8,128)} %get-tuple-element.19.gate_ref) | copy-start | bytes 49156
  197.0 19.5 %copy-start.8 = (f32[2,256,8]{2,1,0:T(8,128)S(1)}, f32[2,256,8]{2,1,0:T(8,128)}, u32[]{:S(2)}) copy-start(f32[2,256,8]{2,1,0:T(8,128)} %get-tuple-element.21.code_ref) | copy-start | bytes 49156
  197.0 19.4 %all-to-all-start.3 = ((bf16[8,128,512]{2,1,0:T(8,128)(2,1)}), bf16[8,128,512]{2,1,0:T(8,128)(2,1)S(1)}, u32[]{:S(2)}, u32[]{:S(2)}) async-start(bf16[8,128,512]{2,1,0:T(8,128)(2,1)} %bitcast.26), calls=%async_computation.3 | async-start | bytes 2097152 | tf_op jit(solution)/shard_map/all_to_all | solution.py:396
Sparse Core Ops, SparseCore 0:
  9.5 86.0 all-gather.2

commit v4 on v3

--- a/solution.py
+++ b/solution.py
@@ -16,6 +16,7 @@
 BF = jnp.bfloat16
 F32 = jnp.float32
 PARAMS = pltpu.CompilerParams(vmem_limit_bytes=40 * 1024 * 1024)
+WIDE = pltpu.CompilerParams(vmem_limit_bytes=60 * 1024 * 1024)
 
 
 def slot_codes(route, choice, placement):
@@ -142,7 +143,7 @@
         functools.partial(gate_kernel, br, last),
         grid_spec=grid_spec,
         out_shape=jax.ShapeDtypeStruct((2, *shape), BF if last else F32),
-        compiler_params=PARAMS,
+        compiler_params=WIDE,
         cost_estimate=pl.CostEstimate(
             flops=len(toks) * depth * cols * (slot_rows + br * learners),
             bytes_accessed=10 * 1024 * 1024,

time: 260 us -> 255 us (0.981)
  local copies, waits for them, and re-layouts: 20.3 us -> 8.29 us
  Pallas kernels: 17.2 us -> 22.5 us
  waiting for transfers between devices: 45.9 us -> 48.8 us
    unnamed x46 -> x24, local copies, waits for them, and re-layouts: 16.5 us -> 4.67 us
    pallas_call x2, Pallas kernels: 10.7 us -> 15.9 us  [gate_hidden(): pl.pallas_call(functools.partial(gate_kernel, br, last), grid_spec=grid_s...]
    all_gather x1, waiting for transfers between devices: 5.96 us -> 9.9 us  [on_device(): deltas = lax.all_gather(flat_deltas, 'z', axis=0, tiled=True)]
  transfers between devices with their start and end apart: 7 -> 7, of which waited for: 5 -> 5; matrix products, arithmetic and copies ran while one was open for 6% -> 5% of each run, Pallas kernels for 4% -> 7%
where the time goes in v4:
time: 255 us; the launch traced here: 254 us
  blocking collectives  125 us (49%)
  waiting for transfers between devices  48.8 us (19%)
  starting transfers between devices  24.5 us (10%)
  Pallas kernels  22.5 us (9%)
  between operations  13.7 us (5%)
  local copies, waits for them, and re-layouts  8.29 us (3%)
  matrix products  6.91 us (3%)
  other arithmetic  4.75 us (2%)
    all_gather x1, blocking collectives, on_device(): packets = lax.all_gather(packet, 'z', axis=0, tiled=False)  42.2 us
    all_to_all x1, blocking collectives, on_device(): lax.all_to_all(partial, 'z', split_axis=0, concat_axis=0, tiled=True)  33.5 us
    all_to_all x1, blocking collectives, on_device(): got = lax.all_to_all(picked, XC, split_axis=0, concat_axis=0, tiled=True)  20.7 us
    pallas_call x2, Pallas kernels, gate_hidden(): pl.pallas_call(functools.partial(gate_kernel, br, last), grid_spec=grid_s...  15.9 us
    all_gather x1, blocking collectives, on_device(): h1 = lax.all_gather(hidden[1], 'dp', axis=0, tiled=False)  14.6 us
    all_to_all x1, waiting for transfers between devices, on_device(): back = lax.all_to_all(out, XC, split_axis=0, concat_axis=0, tiled=True)  14.4 us
    all_gather x1, blocking collectives, on_device(): h0 = lax.all_gather(hidden[0], 'dp', axis=0, tiled=False)  13.7 us
    all_to_all x1, waiting for transfers between devices, on_device(): lax.all_to_all(send_gate.reshape(peers, 2 * nz, cut), XC, split_axis=0, c...  13.7 us
  transfers between devices with their start and end apart: 7, of which 5 were waited for; matrix products, arithmetic and copies ran while one was open for 5% of the time, Pallas kernels for 7%

profile of v4, /device:TPU:2, one launch (start us, length us, event | category | flops | bytes accessed | tf_op | source)
XLA Modules:
  0.0 254.3 jit_solution(9126599586032297582)
XLA Ops:
  6.6 1.0 copy.65
  7.7 1.0 copy.75
  8.6 0.8 pad_maximum_fusion
  9.6 0.1 copy.64
  9.8 0.1 eq.88
  9.9 0.1 reshape.306
  10.0 0.1 select_reduce_fusion.2
  10.2 0.2 select_reduce_fusion.1
  10.4 0.1 convert_element_type.92
  10.7 0.1 copy.74
  11.0 0.1 convert_element_type.104.target_ref
  11.2 42.2 %all-gather = bf16[512,640]{1,0:T(8,128)(2,1)S(1)} all-gather(bf16[32,640]{1,0:T(8,128)(2,1)S(1)} %pad_maximum_fusion.1), channel_id=2, replica_groups=mesh['x'=4,'z'=16,'c'=2,'dp'=4] {'z'}, dimensions={0}, use_global_device_ids=true | all-gather | bytes 696320 | tf_op jit(solution)/shard_map/all_gather | solution.py:305
  53.4 0.4 fusion.2
  53.8 0.2 select_reduce_fusion
  54.1 0.3 slice_add_fusion
  54.4 0.1 copy.68.code_ref
  54.5 1.0 shard_map.109
  55.5 20.7 %all_to_all.25 = bf16[8,144,512]{2,1,0:T(8,128)(2,1)S(1)} all-to-all(bf16[8,144,512]{2,1,0:T(8,128)(2,1)S(1)} %shard_map.109), channel_id=1, replica_groups=mesh['x'=4,'z'=16,'c'=2,'dp'=4] {'x','c'}, dimensions={0} | all-to-all | bytes 2359296 | tf_op jit(solution)/shard_map/all_to_all | solution.py:347
  76.4 6.3 %collective-permute-start.1 = (bf16[8,128,512]{2,1,0:T(8,128)(2,1)S(1)}, bf16[8,128,512]{2,1,0:T(8,128)(2,1)}, u32[]{:S(2)}, u32[]{:S(2)}) collective-permute-start(bf16[8,128,512]{2,1,0:T(8,128)(2,1)S(1)} %slice.65.refs_0_), channel_id=1, source_target_pairs={{0,3},{1,0},{2,1},{3,2},{4,7},{5,4},{6,5},{7,6},{8,11},{9,8},{10,9... | collective-permute-start | bytes 3145736 | tf_op jit(solution)/shard_map/ppermute | solution.py:350
  82.7 1.9 collective-permute-start
  84.8 0.4 broadcast_and_fusion
  85.1 0.9 and.50
  86.0 9.9 %all-gather.3.cloned.1.call-done = bf16[512,4608]{1,0:T(8,128)(2,1)} async-done(((bf16[32,4608]{1,0:T(8,128)(2,1)}), bf16[512,4608]{1,0:T(8,128)(2,1)}) %all-gather.3.cloned.1.call-update) | async-done | bytes 4718608 | tf_op jit(solution)/shard_map/all_gather | solution.py:292
  95.9 4.0 %convolution_convert_fusion = bf16[256,3072]{1,0:T(8,128)(2,1)} fusion(pred[256,512]{1,0:T(32,128)(4,1)S(1)} %and.50, bf16[512,4608]{1,0:T(8,128)(2,1)} %all-gather.3.cloned.1.call-done), kind=kOutput, calls=%fused_computation | convolution fusion | flops 806092800 | bytes 4849664 | tf_op jit(solution)/shard_map/dot_general | solution.py:366
  99.9 5.4 %collective-permute-done.1.refs_2_ = bf16[8,128,512]{2,1,0:T(8,128)(2,1)} collective-permute-done((bf16[8,128,512]{2,1,0:T(8,128)(2,1)S(1)}, bf16[8,128,512]{2,1,0:T(8,128)(2,1)}, u32[]{:S(2)}, u32[]{:S(2)}) %collective-permute-start.1) | collective-permute-done | bytes 1048608 | tf_op jit(solution)/shard_map/ppermute | solution.py:350
  105.3 5.4 %collective-permute-done.refs_1_ = bf16[8,128,512]{2,1,0:T(8,128)(2,1)} collective-permute-done((bf16[8,128,512]{2,1,0:T(8,128)(2,1)S(1)}, bf16[8,128,512]{2,1,0:T(8,128)(2,1)}, u32[]{:S(2)}, u32[]{:S(2)}) %collective-permute-start) | collective-permute-done | bytes 1048608 | tf_op jit(solution)/shard_map/ppermute | solution.py:350
  110.8 4.6 %all-to-all-start.1 = ((bf16[8,32,3072]{2,1,0:T(8,128)(2,1)}), bf16[8,32,3072]{2,1,0:T(8,128)(2,1)S(1)}, u32[]{:S(2)}, u32[]{:S(2)}) async-start(bf16[8,32,3072]{2,1,0:T(8,128)(2,1)} %bitcast.63), calls=%async_computation.1 | async-start | bytes 3145728 | tf_op jit(solution)/shard_map/all_to_all | solution.py:368
  115.4 0.6 pad_add_fusion.where_ref
  116.0 1.9 collective-permute-start.2
  118.3 0.6 broadcast_add_fusion.t_ref
  118.9 2.9 %convolution_convert_fusion.1 = bf16[256,1536]{1,0:T(8,128)(2,1)} fusion(pred[256,512]{1,0:T(32,128)(4,1)S(1)} %and.50, bf16[512,4608]{1,0:T(8,128)(2,1)} %all-gather.3.cloned.1.call-done), kind=kOutput, calls=%fused_computation.2 | convolution fusion | flops 403046400 | bytes 2490368 | tf_op jit(solution)/shard_map/dot_general | solution.py:371
  121.8 13.7 %all-to-all-done.1.d_ref = bf16[8,32,3072]{2,1,0:T(8,128)(2,1)S(1)} async-done(((bf16[8,32,3072]{2,1,0:T(8,128)(2,1)}), bf16[8,32,3072]{2,1,0:T(8,128)(2,1)S(1)}, u32[]{:S(2)}, u32[]{:S(2)}) %all-to-all-start.1) | async-done | bytes 1572896 | tf_op jit(solution)/shard_map/all_to_all | solution.py:368
  135.5 1.2 copy-done.1
  136.7 10.2 %shard_map.110.refs_1_ = f32[2,512,384]{2,1,0:T(8,128)} custom-call(s32[3]{0:T(128)} %pad_add_fusion.where_ref, bf16[2,2048,384]{2,1,0:T(8,128)(2,1)} %bitcast.61, bf16[8,32,3072]{2,1,0:T(8,128)(2,1)} %copy-done.1, s32[2,1,1024]{2,1,0:T(1,128)} %broadcast_add_fusion.t_ref, bf16[8,128,512]{2,1,0:T(8,128)(2,1)} %copy-done.2, ...), custom_call_target="tpu_custom_call" | custom-call | flops 3623878656 | bytes 10485760 | tf_op jit(solution)/shard_map/pallas_call | solution.py:142
  146.8 4.9 %all-to-all-start.2 = ((bf16[8,32,1536]{2,1,0:T(8,128)(2,1)}), bf16[8,32,1536]{2,1,0:T(8,128)(2,1)S(1)}, u32[]{:S(2)}, u32[]{:S(2)}) async-start(bf16[8,32,1536]{2,1,0:T(8,128)(2,1)} %bitcast.23), calls=%async_computation.2 | async-start | bytes 1572864 | tf_op jit(solution)/shard_map/all_to_all | solution.py:376
  151.7 5.8 %shard_map.111 = bf16[2,192,512]{2,1,0:T(8,128)(2,1)} custom-call(s32[1]{0:T(128)} %bitcast.where_ref, bf16[2,2048,384]{2,1,0:T(8,128)(2,1)} %bitcast.62, bf16[8,32,3072]{2,1,0:T(8,128)(2,1)} %copy-done.1, s32[2,1,1024]{2,1,0:T(1,128)} %broadcast_add_fusion.t_ref, bf16[8,128,512]{2,1,0:T(8,128)(2,1)} %collective-permute-done.2.refs_0_, ...), custom_call_target="tpu_custom_call" | custom-call | flops 1207959552 | bytes 10485760 | tf_op jit(solution)/shard_map/pallas_call | solution.py:142
  157.5 1.0 fusion.10
  158.6 14.6 %all_gather.19.h1_ref = bf16[4,192,512]{2,1,0:T(8,128)(2,1)S(1)} all-gather(bf16[1,192,512]{2,1,0:T(8,128)(2,1)S(1)} %get-tuple-element.17), channel_id=1, replica_groups=mesh['x'=4,'z'=16,'c'=2,'dp'=4] {'dp'}, dimensions={0}, use_global_device_ids=true | all-gather | bytes 983040 | tf_op jit(solution)/shard_map/all_gather | solution.py:394
  173.2 13.7 %all_gather.18.h0_ref = bf16[4,192,512]{2,1,0:T(8,128)(2,1)S(1)} all-gather(bf16[1,192,512]{2,1,0:T(8,128)(2,1)S(1)} %get-tuple-element.18), channel_id=1, replica_groups=mesh['x'=4,'z'=16,'c'=2,'dp'=4] {'dp'}, dimensions={0}, use_global_device_ids=true | all-gather | bytes 983040 | tf_op jit(solution)/shard_map/all_gather | solution.py:393
  186.9 1.4 copy-done
  188.3 1.2 shard_map.112.w_ref
  189.6 2.3 shard_map.113
  191.9 4.8 %all-to-all-start.3 = ((bf16[8,128,512]{2,1,0:T(8,128)(2,1)}), bf16[8,128,512]{2,1,0:T(8,128)(2,1)S(1)}, u32[]{:S(2)}, u32[]{:S(2)}) async-start(bf16[8,128,512]{2,1,0:T(8,128)(2,1)} %bitcast.26), calls=%async_computation.3 | async-start | bytes 2097152 | tf_op jit(solution)/shard_map/all_to_all | solution.py:397
  196.7 0.1 convert_element_type.103.target_ref
  196.8 14.4 %all-to-all-done.3 = bf16[8,128,512]{2,1,0:T(8,128)(2,1)S(1)} async-done(((bf16[8,128,512]{2,1,0:T(8,128)(2,1)}), bf16[8,128,512]{2,1,0:T(8,128)(2,1)S(1)}, u32[]{:S(2)}, u32[]{:S(2)}) %all-to-all-start.3) | async-done | bytes 1048608 | tf_op jit(solution)/shard_map/all_to_all | solution.py:397
  211.2 2.1 shard_map.114
  213.3 33.5 %all_to_all.26 = bf16[16,32,512]{2,1,0:T(8,128)(2,1)S(1)} all-to-all(bf16[16,32,512]{2,1,0:T(8,128)(2,1)S(1)} %shard_map.114), channel_id=1, replica_groups=mesh['x'=4,'z'=16,'c'=2,'dp'=4] {'z'}, dimensions={0} | all-to-all | bytes 1048576 | tf_op jit(solution)/shard_map/all_to_all | solution.py:400
  246.7 0.7 reduce_sum.52
  (62 shorter events, 1.6 us)
Async XLA Ops:
  6.5 3.0 %copy-start.8 = (s32[1,32]{1,0:T(1,128)S(1)}, s32[1,32]{1,0:T(1,128)}, u32[]{:S(2)}) copy-start(s32[1,32]{1,0:T(1,128)} %param.19) | copy-start | bytes 388
  6.5 3.0 %copy-start.9 = (s32[1,32]{1,0:T(1,128)S(1)}, s32[1,32]{1,0:T(1,128)}, u32[]{:S(2)}) copy-start(s32[1,32]{1,0:T(1,128)} %param.18) | copy-start | bytes 388
  6.5 3.2 %copy-start.4 = (s32[2,16,8]{1,2,0:T(8,128)S(1)}, s32[2,16,8]{1,2,0:T(8,128)}, u32[]{:S(2)}) copy-start(s32[2,16,8]{1,2,0:T(8,128)} %param.12) | copy-start | bytes 3076
  6.5 3.3 %copy-start.6 = (s32[128,2]{0,1:T(2,128)S(1)}, s32[128,2]{0,1:T(2,128)}, u32[]{:S(2)}) copy-start(s32[128,2]{0,1:T(2,128)} %param.15) | copy-start | bytes 3076
  6.5 3.6 %copy-start.7 = (s32[2,1,128]{2,1,0:T(1,128)S(1)}, s32[2,1,128]{2,1,0:T(1,128)}, u32[]{:S(2)}) copy-start(s32[2,1,128]{2,1,0:T(1,128)} %param.14) | copy-start | bytes 3076
  6.5 4.0 %copy-start.5 = (f32[2,16,8]{1,2,0:T(8,128)S(1)}, f32[2,16,8]{1,2,0:T(8,128)}, u32[]{:S(2)}) copy-start(f32[2,16,8]{1,2,0:T(8,128)} %param.13) | copy-start | bytes 3076
  6.6 4.6 %copy-start.3 = (bf16[2,16,512]{2,1,0:T(8,128)(2,1)S(1)}, bf16[2,16,512]{2,1,0:T(8,128)(2,1)}, u32[]{:S(2)}) copy-start(bf16[2,16,512]{2,1,0:T(8,128)(2,1)} %param.11) | copy-start | bytes 98308
  6.6 89.3 %all-gather.3.cloned.1.call-start = ((), (), s32[]{:S(2)}) async-start(), calls=%async_computation.5 | async-start | bytes 5013504 | tf_op jit(solution)/shard_map/all_gather | solution.py:292
  76.4 23.6 %copy-start.2 = (bf16[8,128,512]{2,1,0:T(8,128)(2,1)}, bf16[8,128,512]{2,1,0:T(8,128)(2,1)S(1)}, u32[]{:S(2)}) copy-start(bf16[8,128,512]{2,1,0:T(8,128)(2,1)S(1)} %slice.65.refs_0_) | copy-start | bytes 3145732
  76.4 29.0 %collective-permute-start.1 = (bf16[8,128,512]{2,1,0:T(8,128)(2,1)S(1)}, bf16[8,128,512]{2,1,0:T(8,128)(2,1)}, u32[]{:S(2)}, u32[]{:S(2)}) collective-permute-start(bf16[8,128,512]{2,1,0:T(8,128)(2,1)S(1)} %slice.65.refs_0_), channel_id=1, source_target_pairs={{0,3},{1,0},{2,1},{3,2},{4,7},{5,4},{6,5},{7,6},{8,11},{9,8},{10,9... | collective-permute-start | bytes 3145736 | tf_op jit(solution)/shard_map/ppermute | solution.py:350
  82.7 28.0 %collective-permute-start = (bf16[8,128,512]{2,1,0:T(8,128)(2,1)S(1)}, bf16[8,128,512]{2,1,0:T(8,128)(2,1)}, u32[]{:S(2)}, u32[]{:S(2)}) collective-permute-start(bf16[8,128,512]{2,1,0:T(8,128)(2,1)S(1)} %slice.65.refs_0_), channel_id=1, source_target_pairs={{0,1},{1,2},{2,3},{3,0},{4,5},{5,6},{6,7},{7,4},{8,9},{9,10},{10,1... | collective-permute-start | bytes 3145736 | tf_op jit(solution)/shard_map/ppermute | solution.py:350
  110.8 24.7 %all-to-all-start.1 = ((bf16[8,32,3072]{2,1,0:T(8,128)(2,1)}), bf16[8,32,3072]{2,1,0:T(8,128)(2,1)S(1)}, u32[]{:S(2)}, u32[]{:S(2)}) async-start(bf16[8,32,3072]{2,1,0:T(8,128)(2,1)} %bitcast.63), calls=%async_computation.1 | async-start | bytes 3145728 | tf_op jit(solution)/shard_map/all_to_all | solution.py:368
  116.0 35.7 %collective-permute-start.2 = (bf16[8,128,512]{2,1,0:T(8,128)(2,1)}, bf16[8,128,512]{2,1,0:T(8,128)(2,1)}, u32[]{:S(2)}, u32[]{:S(2)}) collective-permute-start(bf16[8,128,512]{2,1,0:T(8,128)(2,1)} %copy-done.2), channel_id=1, source_target_pairs={{0,2},{1,3},{2,0},{3,1},{4,6},{5,7},{6,4},{7,5},{8,10},{9,11},{10,... | collective-permute-start | bytes 3145736 | tf_op jit(solution)/shard_map/ppermute | solution.py:350
  135.5 1.2 copy-start.1
  146.8 40.1 %all-to-all-start.2 = ((bf16[8,32,1536]{2,1,0:T(8,128)(2,1)}), bf16[8,32,1536]{2,1,0:T(8,128)(2,1)S(1)}, u32[]{:S(2)}, u32[]{:S(2)}) async-start(bf16[8,32,1536]{2,1,0:T(8,128)(2,1)} %bitcast.23), calls=%async_computation.2 | async-start | bytes 1572864 | tf_op jit(solution)/shard_map/all_to_all | solution.py:376
  186.9 1.4 copy-start
  191.9 19.3 %all-to-all-start.3 = ((bf16[8,128,512]{2,1,0:T(8,128)(2,1)}), bf16[8,128,512]{2,1,0:T(8,128)(2,1)S(1)}, u32[]{:S(2)}, u32[]{:S(2)}) async-start(bf16[8,128,512]{2,1,0:T(8,128)(2,1)} %bitcast.26), calls=%async_computation.3 | async-start | bytes 2097152 | tf_op jit(solution)/shard_map/all_to_all | solution.py:397
Sparse Core Ops, SparseCore 0:
  9.5 86.3 all-gather.2
